TPU v7x, 512 devices: a whole 4x8x8 slice. The times are simulated.
512 devices in a mesh: dom: 32 (over x_lo, z, core), slab: 16 (over y, x_hi).
Axes of the slice: x: 4 (x_hi: 2, x_lo: 2; x = x_hi * 2 + x_lo), y: 8, z: 8, core: 2. Of those that a mesh axis runs over, the one named last changes fastest.
Arguments:
- volume: bfloat16 [16384, 2, 256], P('slab'), may hold values from -6 to 6
- images: bfloat16 [2048, 256, 2, 256], P(('dom', 'slab')), may hold values from -6 to 6
- defocus: float32 [2048], P(('dom', 'slab')), may hold values from 8 to 40
- soft_weights: float32 [2048, 4, 32, 32], P(('dom', 'slab')), may hold values from 0 to 1
- slice_lines: int32 [4, 256], replicated, may hold values from 0 to 16383, as said below
- shift_y: int32 [32], replicated, may hold values from -16 to 15
- shift_x: int32 [32], replicated, may hold values from -16 to 15
Outputs:
- scores: float32 [2048, 4, 32, 32], P(('dom', 'slab'))
- line_update: bfloat16 [16384, 2, 256], P('slab')
Inputs may be any that keep to these rules, and one draw needn't show every extreme that they name: `slice_lines`: in every orientation, each slab s (the lines s * 1024 to (s+1) * 1024 - 1) holds exactly 16 of the 256 slice rows; a line may be named more than once.
All inputs are finite; a program needn't handle non-finite values.
Results may differ from a plain program's by a relative error of at most 0.0055.
Values may be sent and summed in bfloat16 or wider, within the bound.
A program may use at most 128 MiB of HBM per device.

v0:
```python
import math

import jax
import jax.numpy as jnp
from jax import lax
from jax.sharding import PartitionSpec as P


def phase_angles(frequency, shifts, image_side):
    turns = jnp.mod(frequency[..., None] * shifts, image_side)
    return turns.astype(jnp.float32) * (2.0 * math.pi / image_side)


def contrast(defocus, frequency, image_side):
    half_side = image_side // 2
    radius = (frequency[:, None] ** 2 + frequency[None, :] ** 2).astype(jnp.float32) / float(
        half_side * half_side
    )
    aberration = defocus[:, None, None] * radius
    return -(0.995 * jnp.sin(aberration) + 0.1 * jnp.cos(aberration))


def body(volume, images, defocus, soft_weights, slice_lines, shift_y, shift_x):
    highest = lax.Precision.HIGHEST
    slabs = lax.axis_size("slab")
    doms = lax.axis_size("dom")
    slab_index = lax.axis_index("slab")
    lines_dev = volume.shape[0]
    image_side = images.shape[1]
    orient = slice_lines.shape[0]
    shifts_x = shift_x.shape[0]
    shifts_y = shift_y.shape[0]
    owned = image_side // slabs
    frequency = jnp.arange(image_side, dtype=jnp.int32) - image_side // 2
    angle_x = phase_angles(frequency, shift_x, image_side)
    fx_re = jnp.cos(angle_x).astype(jnp.bfloat16)
    fx_im = (-jnp.sin(angle_x)).astype(jnp.bfloat16)
    fx_table = jnp.concatenate(
        [jnp.concatenate([fx_re, fx_im], 1), jnp.concatenate([-fx_im, fx_re], 1)], 0
    )
    row_owner = slice_lines // lines_dev
    owner_marks = (row_owner[:, :, None] == jnp.arange(slabs, dtype=jnp.int32)).astype(jnp.int32)
    earlier = jnp.cumsum(owner_marks, axis=1) - owner_marks
    owner_rank = jnp.sum(earlier * owner_marks, axis=2)
    position = row_owner * owned + owner_rank
    all_rows = jnp.arange(image_side, dtype=jnp.int32)
    matches = (position[:, :, None] == all_rows[None, None, :]).astype(jnp.int32)
    row_order = jnp.sum(matches * all_rows[None, :, None], axis=1)
    sorted_lines = jnp.take_along_axis(slice_lines, row_order, axis=1)
    own_local = (
        lax.dynamic_slice_in_dim(sorted_lines, slab_index * owned, owned, 1)
        - slab_index * lines_dev
    )
    own_rows = volume[own_local]
    contrast_map = contrast(defocus, frequency, image_side)
    arrived = lax.all_gather(own_rows, "slab", axis=1, tiled=True)
    row_index = row_order
    x_rows = images[:, row_index].astype(jnp.float32)
    c_rows = contrast_map[:, row_index]
    slice_re = arrived[:, :, 0].astype(jnp.float32)[None]
    slice_im = arrived[:, :, 1].astype(jnp.float32)[None]
    x_re = x_rows[:, :, :, 0]
    x_im = x_rows[:, :, :, 1]
    q_re = c_rows * (slice_re * x_re + slice_im * x_im)
    q_im = c_rows * (slice_re * x_im - slice_im * x_re)
    q_cat = jnp.concatenate([q_re, q_im], -1).astype(jnp.bfloat16)
    correlated = jnp.einsum("porj,jx->porx", q_cat, fx_table, preferred_element_type=jnp.float32)
    z_re = correlated[..., :shifts_x]
    z_im = correlated[..., shifts_x:]
    angle_y = phase_angles(row_index - image_side // 2, shift_y, image_side)
    fy_re = jnp.cos(angle_y)
    fy_im = -jnp.sin(angle_y)
    running = jnp.einsum("ort,porx->potx", fy_re, z_re, precision=highest) - jnp.einsum(
        "ort,porx->potx", fy_im, z_im, precision=highest
    )
    scores = running / image_side
    back_re = jnp.einsum("potx,kx->potk", soft_weights, jnp.cos(angle_x), precision=highest)
    back_im = jnp.einsum("potx,kx->potk", soft_weights, jnp.sin(angle_x), precision=highest)
    h_stack = jnp.stack([back_re, back_im], 2).astype(jnp.bfloat16)
    row_index = row_order
    angle_y = phase_angles(row_index - image_side // 2, shift_y, image_side)
    phase_re = jnp.cos(angle_y).astype(jnp.bfloat16)
    phase_im = jnp.sin(angle_y).astype(jnp.bfloat16)
    phase_table = jnp.stack(
        [jnp.stack([phase_re, -phase_im], 2), jnp.stack([phase_im, phase_re], 2)], 2
    )
    back_phase = jnp.einsum(
        "ojdct,poctk->pojdk", phase_table, h_stack, preferred_element_type=jnp.float32
    )
    x_rows = images[:, row_index].astype(jnp.float32)
    c_rows = contrast_map[:, row_index]
    c_re = c_rows * x_rows[:, :, :, 0]
    c_im = c_rows * x_rows[:, :, :, 1]
    g_re = back_phase[:, :, :, 0]
    g_im = back_phase[:, :, :, 1]
    t_re = jnp.sum(c_re * g_re - c_im * g_im, axis=0)
    t_im = jnp.sum(c_re * g_im + c_im * g_re, axis=0)
    owned_sum = lax.psum_scatter(
        jnp.stack([t_re, t_im], 2).transpose(1, 0, 2, 3), "slab", scatter_dimension=0, tiled=True
    )
    owned_sum = lax.psum(owned_sum, "dom")
    inserted = owned_sum.transpose(1, 0, 2, 3).reshape(orient * owned, 2 * image_side)
    line_update = (
        jnp.zeros((lines_dev, 2 * image_side), jnp.float32).at[own_local.reshape(-1)].add(inserted)
    )
    particles = images.shape[0] * slabs * doms
    scale_factor = 1.0 / math.sqrt(shifts_y * shifts_x * particles)
    line_update = (
        (line_update * scale_factor).astype(jnp.bfloat16).reshape(lines_dev, 2, image_side)
    )
    return (scores, line_update)


def solution(mesh):
    placed = (
        P("slab", None, None),
        P(("dom", "slab"), None, None, None),
        P(("dom", "slab")),
        P(("dom", "slab"), None, None, None),
        P(),
        P(),
        P(),
    )
    return jax.shard_map(
        body,
        mesh=mesh,
        in_specs=placed,
        out_specs=(P(("dom", "slab"), None, None, None), P("slab", None, None)),
        check_vma=False,
    )
```

profile of v0, /device:TPU:1, one launch (start us, length us, event | category | flops | bytes accessed | tf_op | source)
XLA Modules:
  0.0 512.8 jit_solution(6408843537908931073)
XLA Ops:
  8.0 2.3 reduce-window.6
  11.6 8.8 %gather_fusion.3 = s32[1024]{0:T(1024)S(1)} fusion(s32[4,256]{1,0:T(4,128)} %param.11, s32[1024]{0:T(1024)S(1)} %bitcast.159), kind=kCustom, calls=%fused_computation.3 | custom fusion | bytes 16384 | tf_op jit(solution)/shard_map/jit(take_along_axis)/gather | solution.py:49
  20.6 1.9 gather_fusion.1
  23.4 3.8 fusion.12
  27.9 9.8 %gather_fusion = f32[1024,4,256]{2,1,0:T(4,128)} fusion(f32[4,256,256]{2,0,1:T(4,128)S(1)} %copy.102, s32[1024]{0:T(1024)S(1)} %broadcast_clamp_fusion), kind=kCustom, calls=%fused_computation | custom fusion | bytes 8392704 | tf_op jit(solution)/shard_map/gather | solution.py:59
  37.7 5.0 copy.103
  42.6 16.9 %gather_fusion.2 = bf16[1024,4,2,256]{3,2,1,0:T(2,128)(2,1)} fusion(bf16[4,256,2,256]{3,2,1,0:T(2,128)(2,1)S(1)} %copy-done, s32[1024]{0:T(1024)S(1)} %broadcast_clamp_fusion), kind=kCustom, calls=%fused_computation.2 | custom fusion | bytes 8392704 | tf_op jit(solution)/shard_map/gather | solution.py:58
  59.6 3.1 copy.105
  65.4 4.5 convolution_bitcast_fusion
  69.9 4.3 copy_bitcast_fusion
  74.2 31.4 %all-gather.3.cloned.1.call-done = bf16[4,256,2,256]{3,1,0,2:T(8,128)(2,1)} async-done(((bf16[4,16,2,256]{3,1,0,2:T(8,128)(2,1)}), bf16[4,256,2,256]{3,1,0,2:T(8,128)(2,1)}) %all-gather.3.cloned.1.call-update) | async-done | bytes 1048592 | tf_op jit(solution)/shard_map/all_gather | solution.py:56
  105.6 1.4 fusion.17
  107.0 11.8 %subtract_reduce_fusion = (f32[4,256,256]{2,1,0:T(8,128)S(1)}, f32[4,256,256]{2,1,0:T(8,128)S(1)}, bf16[4,4,256,256]{3,2,1,0:T(8,128)(2,1)S(1)}, bf16[4,4,256,256]{3,2,1,0:T(8,128)(2,1)}) fusion(f32[4,4,256,2,256]{4,2,1,0,3:T(8,128)} %convolution_bitcast_fusion, f32[4,4,256,256]{3,2,1,0:T(8,128)} %bitcast.161, f32[4,4,256,2,256]{4,2,1,0,3:T(8,128)} %copy_bitcast_fusion, ...), kind=kLoop, calls=%fused_computation.15 | loop fusion | flops 20447232 | bytes 33554432 | tf_op jit(solution)/shard_map/reduce_sum | solution.py:96
  118.9 2.6 copy.112
  121.9 1.3 dynamic-slice
  124.3 3.0 fusion
  127.3 1.1 fusion.20
  128.4 156.0 %all-reduce.6.cloned.1.call-done = f32[256,4,2,256]{3,1,2,0:T(4,128)} async-done(((f32[256,4,2,256]{3,1,2,0:T(4,128)}), f32[256,4,2,256]{3,1,2,0:T(4,128)}) %all-reduce.6.cloned.1.call-update) | async-done | bytes 2097168
  284.5 0.9 dynamic-slice_bitcast_fusion
  286.1 1.1 fusion.7
  288.1 213.0 %all-reduce.4.cloned.1.call-done = f32[64,512]{1,0:T(8,128)} async-done(((f32[64,512]{1,0:T(8,128)}), f32[64,512]{1,0:T(8,128)}) %all-reduce.4.cloned.1.call-update) | async-done | bytes 131088 | tf_op jit(solution)/shard_map/psum | solution.py:101
  501.1 1.8 scatter_custom_fusion
  502.9 1.3 multiply_convert_fusion.2
  504.2 2.1 reshape.196
  (55 shorter events, 9.1 us)
Async XLA Ops:
  7.2 35.5 %copy-start = (bf16[4,256,2,256]{3,2,1,0:T(2,128)(2,1)S(1)}, bf16[4,256,2,256]{3,2,1,0:T(2,128)(2,1)}, u32[]{:S(2)}) copy-start(bf16[4,256,2,256]{3,2,1,0:T(2,128)(2,1)} %param.8) | copy-start | bytes 3145732
  7.2 16.2 %copy-start.4 = (f32[4]{0:T(128)S(1)}, f32[4]{0:T(128)}, u32[]{:S(2)}) copy-start(f32[4]{0:T(128)} %param.9) | copy-start | bytes 52
  7.2 98.4 %all-gather.3.cloned.1.call-start = ((), (), s32[]{:S(2)}) async-start(), calls=%async_computation.1 | async-start | bytes 1114112 | tf_op jit(solution)/shard_map/all_gather | solution.py:56
  23.2 261.2 %all-reduce.6.cloned.1.call-start = ((), (), s32[]{:S(2)}) async-start(), calls=%async_computation.2 | async-start | bytes 4194304
  59.6 3.1 copy-start.3
  59.6 4.3 copy-start.1
  59.6 4.3 copy-start.2
  121.5 379.5 %all-reduce.4.cloned.1.call-start = ((), (), s32[]{:S(2)}) async-start(), calls=%async_computation | async-start | bytes 262144 | tf_op jit(solution)/shard_map/psum | solution.py:101
Sparse Core Ops, SparseCore 0:
  23.3 82.2 all-gather.2
  121.7 162.7 all-reduce.5
  287.9 213.0 all-reduce.3
where the time goes:
time: 513 us
  waiting for transfers between devices  400 us (78%)
  local copies, waits for them, and re-layouts  55.8 us (11%)
  other arithmetic  30.4 us (6%)
  between operations  14.7 us (3%)
  matrix products  11.2 us (2%)
    psum x1, waiting for transfers between devices, body(): owned_sum = lax.psum(owned_sum, 'dom')  213 us
    unnamed x4, waiting for transfers between devices  156 us
    all_gather x1, waiting for transfers between devices, body(): arrived = lax.all_gather(own_rows, 'slab', axis=1, tiled=True)  31.4 us
    gather x2, local copies, waits for them, and re-layouts, body(): x_rows = images[:, row_index].astype(jnp.float32)  20 us
    gather x2, local copies, waits for them, and re-layouts, body(): c_rows = contrast_map[:, row_index]  14.7 us
    reduce_sum x1, other arithmetic, body(): t_re = jnp.sum(c_re * g_re - c_im * g_im, axis=0)  11.8 us
  transfers between devices with their start and end apart: 3, of which 3 were waited for; matrix products, arithmetic and copies ran while one was open for 11% of the time, Pallas kernels for 0%

commit v1 on v0

v1 whole, which is shorter than its diff:
```python
import math

import jax
import jax.numpy as jnp
from jax import lax
from jax.experimental import pallas as pl
from jax.experimental.pallas import tpu as pltpu
from jax.sharding import PartitionSpec as P

KS = 256
HALF = KS // 2
P_DEV = 4
LINES = 1024
ORIENT = 4
NT = 32
OWNED = 16
PARTICLES = 2048
SLABS = 16
ZS = 8
XLO = 2
SCALE = 1.0 / math.sqrt(NT * NT * PARTICLES)
F32 = jnp.float32
BF16 = jnp.bfloat16
MESH = pl.DeviceIdType.MESH


def dot(a, b):
    return jnp.dot(a, b, preferred_element_type=F32)


def dot_t(a, b):
    return lax.dot_general(a, b, (((0,), (0,)), ((), ())), preferred_element_type=F32)


def poly_sin_cos(r):
    s = r * r
    sin = r * (1.0 + s * (-1 / 6 + s * (1 / 120 + s * (-1 / 5040 + s * (1 / 362880)))))
    cos = 1.0 + s * (-0.5 + s * (1 / 24 + s * (-1 / 720 + s * (1 / 40320))))
    return sin, cos


def rotate(quadrant, sin, cos):
    q = quadrant & 3
    odd = (q & 1) == 1
    s = jnp.where(odd, cos, sin)
    c = jnp.where(odd, sin, cos)
    s = jnp.where(q >= 2, -s, s)
    c = jnp.where((q == 1) | (q == 2), -c, c)
    return s, c


def turns_sin_cos(turns):
    t = turns & (KS - 1)
    q = (t + KS // 8) >> 6
    r = (t - (q << 6)).astype(F32) * (2.0 * math.pi / KS)
    return rotate(q, *poly_sin_cos(r))


def angle_sin_cos(x):
    n = jnp.floor(x * (2.0 / math.pi) + 0.5)
    r = x - n * 1.5703125
    r = r - n * 4.837512969970703e-4
    r = r - n * 7.549789948768648e-8
    return rotate(n.astype(jnp.int32), *poly_sin_cos(r))


def iota(shape, dim):
    return lax.broadcasted_iota(jnp.int32, shape, dim)


def kernel(
    lines_ref, weights_ref, defocus_ref, sy_ref, sx_ref, volume_hbm, images_hbm,
    scores_ref, update_hbm,
    vbuf, ibuf, split, own, arrived, gather, insert, place_s, place_t,
    fx, ephase, fy, hs, cx, term, sent, landed, zsend, zrecv, tile_f32, tsend, trecv,
    agsend, agrecv, rows, zacc, su,
    in_sem, out_sem, s_send, s_recv, x_send, x_recv, z_send, z_recv, t_send, t_recv, a_send, a_recv,
):
    dom = lax.axis_index("dom")
    slab = lax.axis_index("slab")
    x_lo = dom // 16
    z = (dom // 2) % 8
    c = dom % 2
    zc = z * 2 + c
    partner = (dom + 1 - 2 * c, slab)

    loads = []
    for j in range(2):
        cols = pl.ds(j * 128, 128)
        loads.append(pltpu.make_async_copy(volume_hbm.at[:, :, cols], vbuf.at[j], in_sem.at[j]))
    for j in range(2):
        cols = pl.ds(j * 128, 128)
        loads.append(
            pltpu.make_async_copy(images_hbm.at[:, :, :, cols], ibuf.at[j], in_sem.at[2 + j])
        )
    for load in loads:
        load.start()

    barrier = pltpu.get_barrier_semaphore()

    def tile_peer(k):
        place = lax.rem(x_lo * SLABS + slab + k, XLO * SLABS)
        return (place // SLABS) * 16 + zc, lax.rem(place, SLABS)

    def dom_peer(k):
        return x_lo * 16 + lax.rem(zc + k, 16), slab

    def greet_tile(k, carry):
        pl.semaphore_signal(barrier, inc=1, device_id=tile_peer(k), device_id_type=MESH)
        return carry

    def greet_dom(k, carry):
        pl.semaphore_signal(barrier, inc=1, device_id=dom_peer(k), device_id_type=MESH)
        return carry

    lax.fori_loop(1, XLO * SLABS, greet_tile, 0)
    lax.fori_loop(1, 16, greet_dom, 0)

    lines = lines_ref[...]
    owner = lines >> 10
    local = (lines & (LINES - 1)).astype(F32)
    slab_rows = iota((SLABS, KS), 0)
    marks = jnp.concatenate(
        [(owner[o : o + 1] == slab_rows).astype(F32) for o in range(ORIENT)], 0
    )
    before = (iota((KS, KS), 0) < iota((KS, KS), 1)).astype(F32).astype(BF16)
    earlier = dot(marks.astype(BF16), before) * marks
    ranks = [
        jnp.sum(earlier[o * SLABS : (o + 1) * SLABS], axis=0, keepdims=True).astype(jnp.int32)
        for o in range(ORIENT)
    ]
    own_line = []
    for o in range(ORIENT):
        mine = (owner[o : o + 1] == slab) & (ranks[o] == slab_rows)
        own_line.append(
            jnp.sum(jnp.where(mine, local[o : o + 1], 0.0), axis=1, keepdims=True)
        )
    own_line = jnp.concatenate(own_line, 0).astype(jnp.int32)
    column = iota((ORIENT * OWNED, 2 * LINES), 1)
    gather[0 : ORIENT * OWNED] = (column == 2 * own_line).astype(F32).astype(BF16)
    gather[ORIENT * OWNED :] = (column == 2 * own_line + 1).astype(F32).astype(BF16)

    for j in range(2):
        loads[j].wait()
        picked = dot(gather[...], vbuf.at[j].reshape(2 * LINES, 128)[...]).astype(BF16)
        for part in range(2):
            at = slice(part * KS + j * 128, part * KS + j * 128 + 128)
            for h in range(2):
                first = part * 64 + h * 32
                own[h, :, at] = picked[first : first + 32]

    pl.semaphore_wait(barrier, XLO * SLABS - 1 + 15)

    def slab_copy(k):
        to = lax.rem(slab + k, SLABS)
        return pltpu.make_async_remote_copy(
            src_ref=own.at[c],
            dst_ref=arrived.at[c, slab],
            send_sem=s_send.at[0],
            recv_sem=s_recv.at[0],
            device_id=(dom, to),
            device_id_type=MESH,
        )

    def send_slab(k, carry):
        slab_copy(k).start()
        return carry

    lax.fori_loop(1, SLABS, send_slab, 0)
    arrived[c, slab] = own[c]

    lane = iota((8, 128), 1) % NT
    row_x = jnp.zeros((8, 128), jnp.int32)
    row_y = jnp.zeros((8, 128), jnp.int32)
    for t in range(NT):
        row_x = jnp.where(lane == t, sx_ref[t], row_x)
        row_y = jnp.where(lane == t, sy_ref[t], row_y)
    freq = iota((KS, 128), 0) - HALF
    sin_x, cos_x = turns_sin_cos(freq * row_x[0:1])
    sin_y, cos_y = turns_sin_cos(freq * row_y[0:1])
    wide_lane = iota((KS, 128), 1)
    ephase[0:KS] = jnp.where(wide_lane < NT, cos_y, -sin_y)[:, : 2 * NT].astype(BF16)
    ephase[KS:] = jnp.where(wide_lane < NT, sin_y, cos_y)[:, : 2 * NT].astype(BF16)
    t_cos = cos_x.T[0:NT]
    t_sin = sin_x.T[0:NT]
    table = jnp.concatenate([t_cos, t_sin], 1)
    table_hi = table.astype(BF16)
    table_lo = (table - table_hi.astype(F32)).astype(BF16)
    weights = weights_ref[...]
    weights_hi = weights.astype(BF16)
    weights_lo = (weights - weights_hi.astype(F32)).astype(BF16)
    h = dot(weights_hi, table_hi) + dot(weights_lo, table_hi) + dot(weights_hi, table_lo)
    h = h.astype(BF16).reshape(P_DEV * ORIENT, NT, 2 * KS)
    hs[:, 0:NT] = h[:, :, 0:KS]
    hs[:, NT:] = h[:, :, KS:]
    for o in range(ORIENT):
        rank = ranks[o]
        row = owner[o : o + 1]
        at_t = (rank & 7) * 32 + (rank >> 3) * SLABS + row
        place_t[o] = (iota((KS, KS), 0) == at_t).astype(F32).astype(BF16)

    freq_row = (iota((8, KS), 1) - HALF).astype(F32)
    which = iota((8, KS), 0)
    focus = jnp.zeros((8, KS), F32)
    for p in range(P_DEV):
        focus = jnp.where(which == p, defocus_ref[p], focus)
    sin_d, cos_d = angle_sin_cos(focus * (freq_row * freq_row * (1.0 / (HALF * HALF))))
    sin_col = sin_d.T
    cos_col = cos_d.T
    u_row = 0.1 * sin_d - 0.995 * cos_d
    v_row = -0.995 * sin_d - 0.1 * cos_d
    loads[2].wait()
    loads[3].wait()
    for p in range(P_DEV):
        for j in range(2):
            at = slice(j * 128, j * 128 + 128)
            split[...] = ibuf.at[j, p].reshape(2 * KS, 128)[...].astype(F32)
            ctf = (
                sin_col[:, p : p + 1] * u_row[p : p + 1, at]
                + cos_col[:, p : p + 1] * v_row[p : p + 1, at]
            )
            cx[p, 0, :, at] = ctf * split[pl.ds(0, KS, stride=2), :]
            cx[p, 1, :, at] = ctf * split[pl.ds(1, KS, stride=2), :]

    def placed_term(o):
        for block in range(2):
            at = slice(block * 128, block * 128 + 128)
            low = slice(KS + block * 128, KS + block * 128 + 128)
            t_re = None
            for p in range(P_DEV):
                table_h = hs[p * ORIENT + o]
                g_re = dot(ephase[at], table_h)
                g_im = dot(ephase[low], table_h)
                c_re = cx[p, 0, at]
                c_im = cx[p, 1, at]
                if t_re is None:
                    t_re = c_re * g_re - c_im * g_im
                    t_im = c_re * g_im + c_im * g_re
                else:
                    t_re += c_re * g_re - c_im * g_im
                    t_im += c_re * g_im + c_im * g_re
            term[at, 0:KS] = t_re.astype(BF16)
            term[at, KS:] = t_im.astype(BF16)
        return dot(place_t[o], term[...])

    def pair_copy(j):
        return pltpu.make_async_remote_copy(
            src_ref=sent.at[j],
            dst_ref=landed.at[j],
            send_sem=x_send.at[j],
            recv_sem=x_recv.at[j],
            device_id=partner,
            device_id_type=MESH,
        )

    def z_copy(j, k):
        to = lax.rem(z + k, ZS)
        return pltpu.make_async_remote_copy(
            src_ref=zsend.at[to, j],
            dst_ref=zrecv.at[z, j],
            send_sem=z_send.at[0],
            recv_sem=z_recv.at[0],
            device_id=(x_lo * 16 + to * 2 + c, slab),
            device_id_type=MESH,
        )

    def give(j, carry):
        sent[j] = placed_term(2 * (1 - c) + j).astype(BF16)
        pair_copy(j).start()
        return carry

    lax.fori_loop(0, 2, give, 0)

    def keep(j, carry):
        mine = placed_term(2 * c + j)
        pair_copy(j).wait_recv()
        both = (mine + landed[j].astype(F32)).astype(BF16)
        zsend[:, j] = both.reshape(ZS, NT, 2 * KS)

        def send_z(k, inner):
            z_copy(j, k).start()
            return inner

        lax.fori_loop(1, ZS, send_z, 0)
        zrecv[z, j] = zsend[z, j]
        return carry

    lax.fori_loop(0, 2, keep, 0)

    pltpu.make_async_copy(
        arrived.at[0, pl.ds(0, SLABS - 1)], arrived.at[0, pl.ds(0, SLABS - 1)], s_recv.at[0]
    ).wait()
    forward = pltpu.make_async_remote_copy(
        src_ref=arrived.at[c],
        dst_ref=arrived.at[c],
        send_sem=s_send.at[1],
        recv_sem=s_recv.at[1],
        device_id=partner,
        device_id_type=MESH,
    )
    forward.start()
    for o in range(ORIENT):
        at_s = owner[o : o + 1] * OWNED + ranks[o]
        place_s[o] = (iota((KS, KS), 0) == at_s).astype(F32).astype(BF16)
    group = wide_lane // NT
    for o in range(ORIENT):
        cos_o = jnp.where(group == o, cos_x, 0.0).astype(BF16)
        sin_o = jnp.where(group == o, sin_x, 0.0).astype(BF16)
        fx[o, 0:KS, 0:128] = cos_o
        fx[o, 0:KS, 128:] = -sin_o
        fx[o, KS:, 0:128] = sin_o
        fx[o, KS:, 128:] = cos_o
    table_y = jnp.concatenate([cos_y.T[0:NT], sin_y.T[0:NT]], 1) * (1.0 / KS)
    fy_hi = table_y.astype(BF16)
    fy[0:NT] = fy_hi
    fy[NT:] = (table_y - fy_hi.astype(F32)).astype(BF16)
    insert[...] = gather[...].astype(F32).T.astype(BF16)

    def correlate(half, first):
        for j in range(2):
            o = 2 * half + j
            rows_s = arrived[half, :, j * OWNED : (j + 1) * OWNED, :].reshape(KS, 2 * KS)
            su[...] = dot_t(place_s[o], rows_s)
            for block in range(2):
                at = slice(block * 128, block * 128 + 128)
                for p in range(P_DEV):
                    s_re = su[at, 0:KS]
                    s_im = su[at, KS:]
                    c_re = cx[p, 0, at]
                    c_im = cx[p, 1, at]
                    q_re = (s_re * c_re + s_im * c_im).astype(BF16)
                    q_im = (s_re * c_im - s_im * c_re).astype(BF16)
                    part = dot(q_re, fx[o, 0:KS]) + dot(q_im, fx[o, KS:])
                    if first and j == 0:
                        zacc[p, at] = part
                    else:
                        zacc[p, at] += part

    correlate(c, True)
    forward.wait_recv()
    correlate(1 - c, False)
    for p in range(P_DEV):
        full = jnp.concatenate([zacc[p, :, 0:128], zacc[p, :, 128:]], 0)
        full_hi = full.astype(BF16)
        full_lo = (full - full_hi.astype(F32)).astype(BF16)
        both = dot(fy[...], full_hi)
        scores_ref[p] = both[0:NT] + both[NT:] + dot(fy[0:NT], full_lo)

    pltpu.make_async_copy(zrecv.at[pl.ds(0, ZS - 1)], zrecv.at[pl.ds(0, ZS - 1)], z_recv.at[0]).wait()
    for j in range(2):
        for r in range(2):
            at = slice(r * SLABS, (r + 1) * SLABS)
            total = zrecv[0, j, at].astype(F32)
            for other in range(1, ZS):
                total += zrecv[other, j, at].astype(F32)
            for b in range(4):
                tile_f32[pl.ds(j * 8 + r * 4 + b, SLABS, stride=16), :] = total[
                    :, b * 128 : (b + 1) * 128
                ]
    tsend[...] = tile_f32[...].astype(BF16).reshape(SLABS, 16, 128)

    here = x_lo * SLABS + slab

    def tile_copy(k):
        to = tile_peer(k)
        return pltpu.make_async_remote_copy(
            src_ref=tsend.at[to[1]],
            dst_ref=trecv.at[here],
            send_sem=t_send.at[0],
            recv_sem=t_recv.at[0],
            device_id=to,
            device_id_type=MESH,
        )

    def send_tile(k, carry):
        tile_copy(k).start()
        return carry

    lax.fori_loop(1, XLO * SLABS, send_tile, 0)
    trecv[here] = tsend[slab]
    pltpu.make_async_copy(
        trecv.at[pl.ds(0, XLO * SLABS - 1)], trecv.at[pl.ds(0, XLO * SLABS - 1)], t_recv.at[0]
    ).wait()
    total = trecv[0].astype(F32)
    for other in range(1, XLO * SLABS):
        total += trecv[other].astype(F32)
    agsend[...] = (total * SCALE).astype(BF16)

    def dom_copy(k):
        return pltpu.make_async_remote_copy(
            src_ref=agsend,
            dst_ref=agrecv.at[zc],
            send_sem=a_send.at[0],
            recv_sem=a_recv.at[0],
            device_id=dom_peer(k),
            device_id_type=MESH,
        )

    def send_dom(k, carry):
        dom_copy(k).start()
        return carry

    lax.fori_loop(1, 16, send_dom, 0)
    agrecv[zc] = agsend[...]
    pltpu.make_async_copy(agrecv.at[pl.ds(0, 15)], agrecv.at[pl.ds(0, 15)], a_recv.at[0]).wait()

    tile_f32[...] = agrecv[...].astype(F32).reshape(256, 128)
    for o in range(ORIENT):
        for r in range(2):
            for b in range(4):
                got = tile_f32[
                    pl.ds((o // 2) * 16 + (o % 2) * 8 + r * 4 + b, ZS, stride=32), :
                ]
                first = (b // 2) * 64 + o * OWNED + r * 8
                rows[first : first + 8, (b % 2) * 128 : (b % 2) * 128 + 128] = got
    rows_bf16 = rows[...].astype(BF16)
    placed = dot(insert[...], rows_bf16).astype(BF16)
    outs = []
    for j in range(2):
        vbuf.at[j].reshape(2 * LINES, 128)[...] = placed[:, j * 128 : j * 128 + 128]
        outs.append(
            pltpu.make_async_copy(
                vbuf.at[j], update_hbm.at[:, :, pl.ds(j * 128, 128)], out_sem.at[j]
            )
        )
        outs[j].start()

    pltpu.make_async_copy(
        arrived.at[0, pl.ds(0, SLABS - 1)], arrived.at[0, pl.ds(0, SLABS - 1)], s_send.at[0]
    ).wait()
    forward.wait_send()
    for j in range(2):
        pair_copy(j).wait_send()
    pltpu.make_async_copy(zrecv.at[pl.ds(0, ZS - 1)], zrecv.at[pl.ds(0, ZS - 1)], z_send.at[0]).wait()
    pltpu.make_async_copy(
        trecv.at[pl.ds(0, XLO * SLABS - 1)], trecv.at[pl.ds(0, XLO * SLABS - 1)], t_send.at[0]
    ).wait()
    pltpu.make_async_copy(agrecv.at[pl.ds(0, 15)], agrecv.at[pl.ds(0, 15)], a_send.at[0]).wait()
    for out in outs:
        out.wait()


def body(volume, images, defocus, soft_weights, slice_lines, shift_y, shift_x):
    vmem = pl.BlockSpec(memory_space=pltpu.VMEM)
    smem = pl.BlockSpec(memory_space=pltpu.SMEM)
    hbm = pl.BlockSpec(memory_space=pl.ANY)
    dma = pltpu.SemaphoreType.DMA
    scores, line_update = pl.pallas_call(
        kernel,
        out_shape=(
            jax.ShapeDtypeStruct((P_DEV, NT, ORIENT * NT), F32),
            jax.ShapeDtypeStruct((LINES, 2, KS), BF16),
        ),
        in_specs=[vmem, vmem, smem, smem, smem, hbm, hbm],
        out_specs=(vmem, hbm),
        scratch_shapes=[
            pltpu.VMEM((2, LINES, 2, 128), BF16),
            pltpu.VMEM((2, P_DEV, KS, 2, 128), BF16),
            pltpu.VMEM((2 * KS, 128), F32),
            pltpu.VMEM((2, 2 * OWNED, 2 * KS), BF16),
            pltpu.VMEM((2, SLABS, 2 * OWNED, 2 * KS), BF16),
            pltpu.VMEM((2 * ORIENT * OWNED, 2 * LINES), BF16),
            pltpu.VMEM((2 * LINES, 2 * ORIENT * OWNED), BF16),
            pltpu.VMEM((ORIENT, KS, KS), BF16),
            pltpu.VMEM((ORIENT, KS, KS), BF16),
            pltpu.VMEM((ORIENT, 2 * KS, 256), BF16),
            pltpu.VMEM((2 * KS, 2 * NT), BF16),
            pltpu.VMEM((2 * NT, 2 * KS), BF16),
            pltpu.VMEM((P_DEV * ORIENT, 2 * NT, KS), BF16),
            pltpu.VMEM((P_DEV, 2, KS, KS), F32),
            pltpu.VMEM((KS, 2 * KS), BF16),
            pltpu.VMEM((2, KS, 2 * KS), BF16),
            pltpu.VMEM((2, KS, 2 * KS), BF16),
            pltpu.VMEM((ZS, 2, NT, 2 * KS), BF16),
            pltpu.VMEM((ZS, 2, NT, 2 * KS), BF16),
            pltpu.VMEM((256, 128), F32),
            pltpu.VMEM((SLABS, 16, 128), BF16),
            pltpu.VMEM((XLO * SLABS, 16, 128), BF16),
            pltpu.VMEM((16, 128), BF16),
            pltpu.VMEM((16, 16, 128), BF16),
            pltpu.VMEM((2 * ORIENT * OWNED, KS), F32),
            pltpu.VMEM((P_DEV, KS, 256), F32),
            pltpu.VMEM((KS, 2 * KS), F32),
            dma((4,)),
            dma((2,)),
            dma((2,)),
            dma((2,)),
            dma((2,)),
            dma((2,)),
            dma((1,)),
            dma((1,)),
            dma((1,)),
            dma((1,)),
            dma((1,)),
            dma((1,)),
        ],
        compiler_params=pltpu.CompilerParams(
            collective_id=0, has_side_effects=True, vmem_limit_bytes=48 * 1024 * 1024
        ),
        name="cryo",
    )(
        slice_lines,
        soft_weights.reshape(P_DEV * ORIENT * NT, NT),
        defocus,
        shift_y,
        shift_x,
        volume,
        images,
    )
    scores = scores.reshape(P_DEV, NT, ORIENT, NT).transpose(0, 2, 1, 3)
    return scores, line_update


def solution(mesh):
    placed = (
        P("slab", None, None),
        P(("dom", "slab"), None, None, None),
        P(("dom", "slab")),
        P(("dom", "slab"), None, None, None),
        P(),
        P(),
        P(),
    )
    return jax.shard_map(
        body,
        mesh=mesh,
        in_specs=placed,
        out_specs=(P(("dom", "slab"), None, None, None), P("slab", None, None)),
        check_vma=False,
    )
```

time: 513 us -> 59.8 us (0.12)
  waiting for transfers between devices: 400 us -> 0 us
  Pallas kernels: 0 us -> 52.2 us
  local copies, waits for them, and re-layouts: 55.8 us -> 6.61 us
  other arithmetic: 30.4 us -> 0 us
  between operations: 14.7 us -> 0.68 us
  matrix products: 11.2 us -> 0 us
    psum x1 -> x0, waiting for transfers between devices: 213 us -> none  [body(): owned_sum = lax.psum(owned_sum, 'dom')]
    unnamed x4 -> x0, waiting for transfers between devices: 156 us -> none
    pallas_call x0 -> x1, Pallas kernels: none -> 52.2 us  [body(): pl.pallas_call(kernel, out_shape=(jax.ShapeDtypeStruct((P_DEV, NT, ORIENT...]
    gather x8 -> x0, local copies, waits for them, and re-layouts: 46.1 us -> none  [the longest x2 20 us: body(): x_rows = images[:, row_index].astype(jnp.float32)]
    all_gather x1 -> x0, waiting for transfers between devices: 31.4 us -> none  [body(): arrived = lax.all_gather(own_rows, 'slab', axis=1, tiled=True)]
    reduce_sum x3 -> x0, other arithmetic: 12.1 us -> none  [the longest x1 11.8 us: body(): t_re = jnp.sum(c_re * g_re - c_im * g_im, axis=0)]
    dot_general x6 -> x0, matrix products: 11.2 us -> none  [the longest x1 4.51 us: body(): jnp.einsum('ojdct,poctk->pojdk', phase_table, h_stack, preferred_element_...]
    convert_element_type x6 -> x0, other arithmetic: 7.73 us -> none  [the longest x1 4.26 us: body(): x_rows = images[:, row_index].astype(jnp.float32)]
  transfers between devices with their start and end apart: 3 -> 0, of which waited for: 3 -> 0; matrix products, arithmetic and copies ran while one was open for 11% -> 0% of each run, Pallas kernels for 0% -> 0%
where the time goes in v1:
time: 59.8 us; the launch traced here: 59.5 us
  Pallas kernels  52.2 us (87%)
  local copies, waits for them, and re-layouts  6.61 us (11%)
  between operations  0.68 us (1%)
    pallas_call x1, Pallas kernels, body(): pl.pallas_call(kernel, out_shape=(jax.ShapeDtypeStruct((P_DEV, NT, ORIENT...  52.2 us
    unnamed x15, local copies, waits for them, and re-layouts  5.72 us

profile of v1, /device:TPU:1, one launch (start us, length us, event | category | flops | bytes accessed | tf_op | source)
XLA Modules:
  0.0 59.5 jit_solution(16958923805744278868)
XLA Ops:
  0.6 0.0 copy-start.5
  0.6 0.0 copy-start.6
  0.7 0.0 copy-start.4
  0.7 0.6 %copy-done.5 = s32[32]{0:T(128)S(1)} copy-done((s32[32]{0:T(128)S(1)}, s32[32]{0:T(128)}, u32[]{:S(2)}) %copy-start.5) | copy-done | bytes 152
  1.3 0.0 copy-done.6
  1.3 0.0 copy-done.4
  1.3 0.0 copy-start
  1.3 1.2 %copy-done = bf16[1024,2,256]{2,1,0:T(2,128)(2,1)S(1)} copy-done((bf16[1024,2,256]{2,1,0:T(2,128)(2,1)S(1)}, bf16[1024,2,256]{2,1,0:T(2,128)(2,1)}, u32[]{:S(2)}) %copy-start) | copy-done | bytes 1048600
  2.5 0.0 copy-start.1
  2.5 1.2 %copy-done.1 = bf16[4,256,2,256]{3,2,1,0:T(2,128)(2,1)S(1)} copy-done((bf16[4,256,2,256]{3,2,1,0:T(2,128)(2,1)S(1)}, bf16[4,256,2,256]{3,2,1,0:T(2,128)(2,1)}, u32[]{:S(2)}) %copy-start.1) | copy-done | bytes 1048600
  3.8 0.0 copy-start.2
  3.8 0.9 %copy-done.2 = f32[4,4,32,32]{3,2,1,0:T(8,128)S(1)} copy-done((f32[4,4,32,32]{3,2,1,0:T(8,128)S(1)}, f32[4,4,32,32]{3,2,1,0:T(8,128)}, u32[]{:S(2)}) %copy-start.2) | copy-done | bytes 65560
  4.7 0.0 copy-start.3
  4.7 0.7 %copy-done.3 = s32[4,256]{1,0:T(4,128)S(1)} copy-done((s32[4,256]{1,0:T(4,128)S(1)}, s32[4,256]{1,0:T(4,128)}, u32[]{:S(2)}) %copy-start.3) | copy-done | bytes 4120
  5.4 52.2 %cryo.1 = (f32[4,32,128]{2,1,0:T(8,128)S(1)}, bf16[1024,2,256]{2,1,0:T(2,128)(2,1)S(1)}) custom-call(s32[4,256]{1,0:T(4,128)S(1)} %copy-done.3, f32[512,32]{1,0:T(8,128)S(1)} %bitcast.4, f32[4]{0:T(128)S(1)} %copy-done.4, s32[32]{0:T(128)S(1)} %copy-done.5, s32[32]{0:T(128)S(1)} %copy-done.6, bf16[1024,2,256]{2,1,0:T(2,128)(2,1)S(1)} %copy-done, ...), custom_call_target="tpu_custom_call" | custom-call | tf_op jit(solution)/shard_map/cryo/pallas_call | solution.py:448
  57.6 0.2 reshape.11
  57.8 0.7 %copy.11 = f32[4,32,4,32]{3,1,2,0:T(8,128)} copy(f32[4,32,4,32]{3,2,1,0:T(4,128)S(1)} %reshape.11) | data formatting | bytes 131072 | tf_op jit(solution)/shard_map/reshape | solution.py:510
  58.5 1.0 %copy.13 = bf16[1024,2,256]{2,1,0:T(2,128)(2,1)} copy(bf16[1024,2,256]{2,1,0:T(2,128)(2,1)S(1)} %get-tuple-element.9) | data formatting | bytes 2097152
Async XLA Ops:
  0.6 0.7 %copy-start.5 = (s32[32]{0:T(128)S(1)}, s32[32]{0:T(128)}, u32[]{:S(2)}) copy-start(s32[32]{0:T(128)} %sy_ref.1) | copy-start | bytes 388
  0.6 0.7 %copy-start.6 = (s32[32]{0:T(128)S(1)}, s32[32]{0:T(128)}, u32[]{:S(2)}) copy-start(s32[32]{0:T(128)} %sx_ref.1) | copy-start | bytes 388
  0.7 0.7 %copy-start.4 = (f32[4]{0:T(128)S(1)}, f32[4]{0:T(128)}, u32[]{:S(2)}) copy-start(f32[4]{0:T(128)} %defocus_ref.1) | copy-start | bytes 52
  1.3 1.2 %copy-start = (bf16[1024,2,256]{2,1,0:T(2,128)(2,1)S(1)}, bf16[1024,2,256]{2,1,0:T(2,128)(2,1)}, u32[]{:S(2)}) copy-start(bf16[1024,2,256]{2,1,0:T(2,128)(2,1)} %volume_hbm.1) | copy-start | bytes 3145732
  2.5 1.2 %copy-start.1 = (bf16[4,256,2,256]{3,2,1,0:T(2,128)(2,1)S(1)}, bf16[4,256,2,256]{3,2,1,0:T(2,128)(2,1)}, u32[]{:S(2)}) copy-start(bf16[4,256,2,256]{3,2,1,0:T(2,128)(2,1)} %images_hbm.1) | copy-start | bytes 3145732
  3.8 0.9 %copy-start.2 = (f32[4,4,32,32]{3,2,1,0:T(8,128)S(1)}, f32[4,4,32,32]{3,2,1,0:T(8,128)}, u32[]{:S(2)}) copy-start(f32[4,4,32,32]{3,2,1,0:T(8,128)} %param.10) | copy-start | bytes 196612
  4.7 0.7 %copy-start.3 = (s32[4,256]{1,0:T(4,128)S(1)}, s32[4,256]{1,0:T(4,128)}, u32[]{:S(2)}) copy-start(s32[4,256]{1,0:T(4,128)} %lines_ref.1) | copy-start | bytes 12292

commit v2 on v1

--- a/solution.py
+++ b/solution.py
@@ -17,6 +17,7 @@
 PARTICLES = 2048
 SLABS = 16
 ZS = 8
+YS = 8
 XLO = 2
 SCALE = 1.0 / math.sqrt(NT * NT * PARTICLES)
 F32 = jnp.float32
@@ -69,12 +70,14 @@
 
 
 def kernel(
-    lines_ref, weights_ref, defocus_ref, sy_ref, sx_ref, volume_hbm, images_hbm,
+    lines_hbm, weights_hbm, defocus_hbm, sy_hbm, sx_hbm, volume_hbm, images_hbm,
     scores_ref, update_hbm,
+    lines_ref, weights_ref, defocus_ref, sy_ref, sx_ref,
     vbuf, ibuf, split, own, arrived, gather, insert, place_s, place_t,
-    fx, ephase, fy, hs, cx, term, sent, landed, zsend, zrecv, tile_f32, tsend, trecv,
-    agsend, agrecv, rows, zacc, su,
-    in_sem, out_sem, s_send, s_recv, x_send, x_recv, z_send, z_recv, t_send, t_recv, a_send, a_recv,
+    fx, ephase, fy, hs, cx, term, sent, landed, xsend, xrecv, zsend, zrecv, ysend, yrecv,
+    agsend, agrecv, tile_z, tile_f32, rows, zacc, su,
+    small_sem, in_sem, out_sem, s_send, s_recv, p_send, p_recv, x_send, x_recv, z_send, z_recv,
+    y_send, y_recv, a_send, a_recv,
 ):
     dom = lax.axis_index("dom")
     slab = lax.axis_index("slab")
@@ -83,7 +86,24 @@
     c = dom % 2
     zc = z * 2 + c
     partner = (dom + 1 - 2 * c, slab)
-
+    y = slab // 2
+    x_hi = slab % 2
+    x = x_hi * 2 + x_lo
+
+    small = [
+        pltpu.make_async_copy(src, dst, small_sem.at[i])
+        for i, (src, dst) in enumerate(
+            (
+                (lines_hbm, lines_ref),
+                (sx_hbm, sx_ref),
+                (sy_hbm, sy_ref),
+                (defocus_hbm, defocus_ref),
+                (weights_hbm, weights_ref),
+            )
+        )
+    ]
+    for load in small:
+        load.start()
     loads = []
     for j in range(2):
         cols = pl.ds(j * 128, 128)
@@ -98,24 +118,37 @@
 
     barrier = pltpu.get_barrier_semaphore()
 
-    def tile_peer(k):
-        place = lax.rem(x_lo * SLABS + slab + k, XLO * SLABS)
-        return (place // SLABS) * 16 + zc, lax.rem(place, SLABS)
+    def slab_peer(k):
+        return dom, lax.rem(slab + k, SLABS)
+
+    def x_peer(k):
+        to = lax.rem(x + k, 4)
+        return (to % 2) * 16 + zc, y * 2 + to // 2
+
+    def y_peer(k):
+        to = lax.rem(x_lo * YS + y + k, XLO * YS)
+        return (to // YS) * 16 + zc, (to % YS) * 2 + x_hi
 
     def dom_peer(k):
         return x_lo * 16 + lax.rem(zc + k, 16), slab
 
-    def greet_tile(k, carry):
-        pl.semaphore_signal(barrier, inc=1, device_id=tile_peer(k), device_id_type=MESH)
-        return carry
-
-    def greet_dom(k, carry):
-        pl.semaphore_signal(barrier, inc=1, device_id=dom_peer(k), device_id_type=MESH)
-        return carry
-
-    lax.fori_loop(1, XLO * SLABS, greet_tile, 0)
-    lax.fori_loop(1, 16, greet_dom, 0)
-
+    def greet(peer):
+        pl.semaphore_signal(barrier, inc=1, device_id=peer, device_id_type=MESH)
+
+    def greet_both(k, carry):
+        greet(slab_peer(k))
+        greet(dom_peer(k))
+        return carry
+
+    def greet_other(k, carry):
+        greet(((1 - x_lo) * 16 + zc, k * 2 + x_hi))
+        return carry
+
+    lax.fori_loop(1, SLABS, greet_both, 0)
+    lax.fori_loop(0, YS, greet_other, 0)
+    greet(((1 - x_lo) * 16 + zc, y * 2 + 1 - x_hi))
+
+    small[0].wait()
     lines = lines_ref[...]
     owner = lines >> 10
     local = (lines & (LINES - 1)).astype(F32)
@@ -136,29 +169,27 @@
             jnp.sum(jnp.where(mine, local[o : o + 1], 0.0), axis=1, keepdims=True)
         )
     own_line = jnp.concatenate(own_line, 0).astype(jnp.int32)
-    column = iota((ORIENT * OWNED, 2 * LINES), 1)
-    gather[0 : ORIENT * OWNED] = (column == 2 * own_line).astype(F32).astype(BF16)
-    gather[ORIENT * OWNED :] = (column == 2 * own_line + 1).astype(F32).astype(BF16)
+    half_line = jnp.where(c == 0, own_line[0 : 2 * OWNED], own_line[2 * OWNED :])
+    column = iota((2 * OWNED, 2 * LINES), 1)
+    gather[0 : 2 * OWNED] = (column == 2 * half_line).astype(F32).astype(BF16)
+    gather[2 * OWNED :] = (column == 2 * half_line + 1).astype(F32).astype(BF16)
 
     for j in range(2):
         loads[j].wait()
         picked = dot(gather[...], vbuf.at[j].reshape(2 * LINES, 128)[...]).astype(BF16)
         for part in range(2):
             at = slice(part * KS + j * 128, part * KS + j * 128 + 128)
-            for h in range(2):
-                first = part * 64 + h * 32
-                own[h, :, at] = picked[first : first + 32]
-
-    pl.semaphore_wait(barrier, XLO * SLABS - 1 + 15)
+            own[:, at] = picked[part * 32 : part * 32 + 32]
+
+    pl.semaphore_wait(barrier, 2 * (SLABS - 1) + YS + 1)
 
     def slab_copy(k):
-        to = lax.rem(slab + k, SLABS)
         return pltpu.make_async_remote_copy(
-            src_ref=own.at[c],
+            src_ref=own,
             dst_ref=arrived.at[c, slab],
             send_sem=s_send.at[0],
             recv_sem=s_recv.at[0],
-            device_id=(dom, to),
+            device_id=slab_peer(k),
             device_id_type=MESH,
         )
 
@@ -167,8 +198,10 @@
         return carry
 
     lax.fori_loop(1, SLABS, send_slab, 0)
-    arrived[c, slab] = own[c]
-
+    arrived[c, slab] = own[...]
+
+    small[1].wait()
+    small[2].wait()
     lane = iota((8, 128), 1) % NT
     row_x = jnp.zeros((8, 128), jnp.int32)
     row_y = jnp.zeros((8, 128), jnp.int32)
@@ -186,6 +219,7 @@
     table = jnp.concatenate([t_cos, t_sin], 1)
     table_hi = table.astype(BF16)
     table_lo = (table - table_hi.astype(F32)).astype(BF16)
+    small[4].wait()
     weights = weights_ref[...]
     weights_hi = weights.astype(BF16)
     weights_lo = (weights - weights_hi.astype(F32)).astype(BF16)
@@ -196,12 +230,13 @@
     for o in range(ORIENT):
         rank = ranks[o]
         row = owner[o : o + 1]
-        at_t = (rank & 7) * 32 + (rank >> 3) * SLABS + row
+        at_t = (row & 1) * 128 + (rank >> 3) * 64 + (rank & 7) * YS + (row >> 1)
         place_t[o] = (iota((KS, KS), 0) == at_t).astype(F32).astype(BF16)
 
     freq_row = (iota((8, KS), 1) - HALF).astype(F32)
     which = iota((8, KS), 0)
     focus = jnp.zeros((8, KS), F32)
+    small[3].wait()
     for p in range(P_DEV):
         focus = jnp.where(which == p, defocus_ref[p], focus)
     sin_d, cos_d = angle_sin_cos(focus * (freq_row * freq_row * (1.0 / (HALF * HALF))))
@@ -247,17 +282,27 @@
         return pltpu.make_async_remote_copy(
             src_ref=sent.at[j],
             dst_ref=landed.at[j],
+            send_sem=p_send.at[j],
+            recv_sem=p_recv.at[j],
+            device_id=partner,
+            device_id_type=MESH,
+        )
+
+    def x_copy(j, k):
+        return pltpu.make_async_remote_copy(
+            src_ref=xsend.at[j, lax.rem(x + k, 4)],
+            dst_ref=xrecv.at[j, x],
             send_sem=x_send.at[j],
             recv_sem=x_recv.at[j],
-            device_id=partner,
+            device_id=x_peer(k),
             device_id_type=MESH,
         )
 
     def z_copy(j, k):
         to = lax.rem(z + k, ZS)
         return pltpu.make_async_remote_copy(
-            src_ref=zsend.at[to, j],
-            dst_ref=zrecv.at[z, j],
+            src_ref=zsend.at[j, to],
+            dst_ref=zrecv.at[j, z],
             send_sem=z_send.at[0],
             recv_sem=z_recv.at[0],
             device_id=(x_lo * 16 + to * 2 + c, slab),
@@ -275,14 +320,14 @@
         mine = placed_term(2 * c + j)
         pair_copy(j).wait_recv()
         both = (mine + landed[j].astype(F32)).astype(BF16)
-        zsend[:, j] = both.reshape(ZS, NT, 2 * KS)
-
-        def send_z(k, inner):
-            z_copy(j, k).start()
+        xsend[j] = both.reshape(4, 64, 2 * KS)
+
+        def send_x(k, inner):
+            x_copy(j, k).start()
             return inner
 
-        lax.fori_loop(1, ZS, send_z, 0)
-        zrecv[z, j] = zsend[z, j]
+        lax.fori_loop(1, 4, send_x, 0)
+        xrecv[j, x] = xsend[j, x]
         return carry
 
     lax.fori_loop(0, 2, keep, 0)
@@ -314,7 +359,6 @@
     fy_hi = table_y.astype(BF16)
     fy[0:NT] = fy_hi
     fy[NT:] = (table_y - fy_hi.astype(F32)).astype(BF16)
-    insert[...] = gather[...].astype(F32).T.astype(BF16)
 
     def correlate(half, first):
         for j in range(2):
@@ -337,8 +381,61 @@
                         zacc[p, at] += part
 
     correlate(c, True)
+
+    def pass_on(j, carry):
+        pltpu.make_async_copy(
+            xrecv.at[j, pl.ds(0, 3)], xrecv.at[j, pl.ds(0, 3)], x_recv.at[j]
+        ).wait()
+        for part in range(2):
+            at = slice(part * KS, part * KS + KS)
+            total = xrecv[j, 0, :, at].astype(F32)
+            for other in range(1, 4):
+                total += xrecv[j, other, :, at].astype(F32)
+            tile_z[:, part * YS : part * YS + YS] = total.reshape(ZS, YS, KS)
+        zsend[j] = tile_z[...].astype(BF16)
+
+        def send_z(k, inner):
+            z_copy(j, k).start()
+            return inner
+
+        lax.fori_loop(1, ZS, send_z, 0)
+        zrecv[j, z] = zsend[j, z]
+        return carry
+
+    lax.fori_loop(0, 2, pass_on, 0)
     forward.wait_recv()
     correlate(1 - c, False)
+    pltpu.make_async_copy(
+        zrecv.at[:, pl.ds(0, ZS - 1)], zrecv.at[:, pl.ds(0, ZS - 1)], z_recv.at[0]
+    ).wait()
+    for j in range(2):
+        total = zrecv[j, 0].astype(F32)
+        for other in range(1, ZS):
+            total += zrecv[j, other].astype(F32)
+        for part in range(2):
+            for b in range(2):
+                tile_f32[pl.ds(j * 4 + part * 2 + b, YS, stride=8), :] = total[
+                    part * YS : part * YS + YS, b * 128 : b * 128 + 128
+                ]
+    ysend[...] = tile_f32[0 : YS * 8].reshape(YS, 8, 128)
+
+    def y_copy(k):
+        to = lax.rem(x_lo * YS + y + k, XLO * YS)
+        return pltpu.make_async_remote_copy(
+            src_ref=ysend.at[to % YS],
+            dst_ref=yrecv.at[x_lo * YS + y],
+            send_sem=y_send.at[0],
+            recv_sem=y_recv.at[0],
+            device_id=y_peer(k),
+            device_id_type=MESH,
+        )
+
+    def send_y(k, carry):
+        y_copy(k).start()
+        return carry
+
+    lax.fori_loop(1, XLO * YS, send_y, 0)
+    yrecv[x_lo * YS + y] = ysend[y]
     for p in range(P_DEV):
         full = jnp.concatenate([zacc[p, :, 0:128], zacc[p, :, 128:]], 0)
         full_hi = full.astype(BF16)
@@ -346,45 +443,19 @@
         both = dot(fy[...], full_hi)
         scores_ref[p] = both[0:NT] + both[NT:] + dot(fy[0:NT], full_lo)
 
-    pltpu.make_async_copy(zrecv.at[pl.ds(0, ZS - 1)], zrecv.at[pl.ds(0, ZS - 1)], z_recv.at[0]).wait()
-    for j in range(2):
-        for r in range(2):
-            at = slice(r * SLABS, (r + 1) * SLABS)
-            total = zrecv[0, j, at].astype(F32)
-            for other in range(1, ZS):
-                total += zrecv[other, j, at].astype(F32)
-            for b in range(4):
-                tile_f32[pl.ds(j * 8 + r * 4 + b, SLABS, stride=16), :] = total[
-                    :, b * 128 : (b + 1) * 128
-                ]
-    tsend[...] = tile_f32[...].astype(BF16).reshape(SLABS, 16, 128)
-
-    here = x_lo * SLABS + slab
-
-    def tile_copy(k):
-        to = tile_peer(k)
-        return pltpu.make_async_remote_copy(
-            src_ref=tsend.at[to[1]],
-            dst_ref=trecv.at[here],
-            send_sem=t_send.at[0],
-            recv_sem=t_recv.at[0],
-            device_id=to,
-            device_id_type=MESH,
-        )
-
-    def send_tile(k, carry):
-        tile_copy(k).start()
-        return carry
-
-    lax.fori_loop(1, XLO * SLABS, send_tile, 0)
-    trecv[here] = tsend[slab]
+    line_row = jnp.concatenate([2 * own_line, 2 * own_line + 1], 0).astype(F32)
+    line_row = jnp.broadcast_to(line_row, (128, 128)).T[0:1].astype(jnp.int32)
+    insert[...] = (iota((2 * LINES, 128), 0) == line_row).astype(F32).astype(BF16)
     pltpu.make_async_copy(
-        trecv.at[pl.ds(0, XLO * SLABS - 1)], trecv.at[pl.ds(0, XLO * SLABS - 1)], t_recv.at[0]
+        yrecv.at[pl.ds(0, XLO * YS - 1)], yrecv.at[pl.ds(0, XLO * YS - 1)], y_recv.at[0]
     ).wait()
-    total = trecv[0].astype(F32)
-    for other in range(1, XLO * SLABS):
-        total += trecv[other].astype(F32)
-    agsend[...] = (total * SCALE).astype(BF16)
+    sums = []
+    for half in range(XLO):
+        total = yrecv[half * YS]
+        for other in range(1, YS):
+            total += yrecv[half * YS + other]
+        sums.append(total * SCALE)
+    agsend[...] = jnp.concatenate(sums, 0).astype(BF16)
 
     def dom_copy(k):
         return pltpu.make_async_remote_copy(
@@ -409,7 +480,7 @@
         for r in range(2):
             for b in range(4):
                 got = tile_f32[
-                    pl.ds((o // 2) * 16 + (o % 2) * 8 + r * 4 + b, ZS, stride=32), :
+                    pl.ds((o // 2) * 16 + r * 8 + (o % 2) * 4 + b, ZS, stride=32), :
                 ]
                 first = (b // 2) * 64 + o * OWNED + r * 8
                 rows[first : first + 8, (b % 2) * 128 : (b % 2) * 128 + 128] = got
@@ -431,9 +502,15 @@
     forward.wait_send()
     for j in range(2):
         pair_copy(j).wait_send()
-    pltpu.make_async_copy(zrecv.at[pl.ds(0, ZS - 1)], zrecv.at[pl.ds(0, ZS - 1)], z_send.at[0]).wait()
+    for j in range(2):
+        pltpu.make_async_copy(
+            xrecv.at[j, pl.ds(0, 3)], xrecv.at[j, pl.ds(0, 3)], x_send.at[j]
+        ).wait()
     pltpu.make_async_copy(
-        trecv.at[pl.ds(0, XLO * SLABS - 1)], trecv.at[pl.ds(0, XLO * SLABS - 1)], t_send.at[0]
+        zrecv.at[:, pl.ds(0, ZS - 1)], zrecv.at[:, pl.ds(0, ZS - 1)], z_send.at[0]
+    ).wait()
+    pltpu.make_async_copy(
+        yrecv.at[pl.ds(0, XLO * YS - 1)], yrecv.at[pl.ds(0, XLO * YS - 1)], y_send.at[0]
     ).wait()
     pltpu.make_async_copy(agrecv.at[pl.ds(0, 15)], agrecv.at[pl.ds(0, 15)], a_send.at[0]).wait()
     for out in outs:
@@ -442,7 +519,6 @@
 
 def body(volume, images, defocus, soft_weights, slice_lines, shift_y, shift_x):
     vmem = pl.BlockSpec(memory_space=pltpu.VMEM)
-    smem = pl.BlockSpec(memory_space=pltpu.SMEM)
     hbm = pl.BlockSpec(memory_space=pl.ANY)
     dma = pltpu.SemaphoreType.DMA
     scores, line_update = pl.pallas_call(
@@ -451,15 +527,20 @@
             jax.ShapeDtypeStruct((P_DEV, NT, ORIENT * NT), F32),
             jax.ShapeDtypeStruct((LINES, 2, KS), BF16),
         ),
-        in_specs=[vmem, vmem, smem, smem, smem, hbm, hbm],
+        in_specs=[hbm] * 7,
         out_specs=(vmem, hbm),
         scratch_shapes=[
+            pltpu.VMEM((ORIENT, KS), jnp.int32),
+            pltpu.VMEM((P_DEV * ORIENT * NT, NT), F32),
+            pltpu.SMEM((P_DEV,), F32),
+            pltpu.SMEM((NT,), jnp.int32),
+            pltpu.SMEM((NT,), jnp.int32),
             pltpu.VMEM((2, LINES, 2, 128), BF16),
             pltpu.VMEM((2, P_DEV, KS, 2, 128), BF16),
             pltpu.VMEM((2 * KS, 128), F32),
-            pltpu.VMEM((2, 2 * OWNED, 2 * KS), BF16),
+            pltpu.VMEM((2 * OWNED, 2 * KS), BF16),
             pltpu.VMEM((2, SLABS, 2 * OWNED, 2 * KS), BF16),
-            pltpu.VMEM((2 * ORIENT * OWNED, 2 * LINES), BF16),
+            pltpu.VMEM((4 * OWNED, 2 * LINES), BF16),
             pltpu.VMEM((2 * LINES, 2 * ORIENT * OWNED), BF16),
             pltpu.VMEM((ORIENT, KS, KS), BF16),
             pltpu.VMEM((ORIENT, KS, KS), BF16),
@@ -471,17 +552,23 @@
             pltpu.VMEM((KS, 2 * KS), BF16),
             pltpu.VMEM((2, KS, 2 * KS), BF16),
             pltpu.VMEM((2, KS, 2 * KS), BF16),
-            pltpu.VMEM((ZS, 2, NT, 2 * KS), BF16),
-            pltpu.VMEM((ZS, 2, NT, 2 * KS), BF16),
-            pltpu.VMEM((256, 128), F32),
-            pltpu.VMEM((SLABS, 16, 128), BF16),
-            pltpu.VMEM((XLO * SLABS, 16, 128), BF16),
+            pltpu.VMEM((2, 4, 64, 2 * KS), BF16),
+            pltpu.VMEM((2, 4, 64, 2 * KS), BF16),
+            pltpu.VMEM((2, ZS, 16, KS), BF16),
+            pltpu.VMEM((2, ZS, 16, KS), BF16),
+            pltpu.VMEM((YS, 8, 128), F32),
+            pltpu.VMEM((XLO * YS, 8, 128), F32),
             pltpu.VMEM((16, 128), BF16),
             pltpu.VMEM((16, 16, 128), BF16),
+            pltpu.VMEM((ZS, 16, KS), F32),
+            pltpu.VMEM((256, 128), F32),
             pltpu.VMEM((2 * ORIENT * OWNED, KS), F32),
             pltpu.VMEM((P_DEV, KS, 256), F32),
             pltpu.VMEM((KS, 2 * KS), F32),
+            dma((5,)),
             dma((4,)),
+            dma((2,)),
+            dma((2,)),
             dma((2,)),
             dma((2,)),
             dma((2,)),

time: 59.8 us -> 58.1 us (0.972)
  Pallas kernels: 52.2 us -> 50.5 us
    pallas_call x1, Pallas kernels: 52.2 us -> 50.5 us  [body(): pl.pallas_call(kernel, out_shape=(jax.ShapeDtypeStruct((P_DEV, NT, ORIENT...]
where the time goes in v2:
time: 58.1 us; the launch traced here: 57.8 us
  Pallas kernels  50.5 us (87%)
  local copies, waits for them, and re-layouts  6.61 us (11%)
  between operations  0.68 us (1%)
    pallas_call x1, Pallas kernels, body(): pl.pallas_call(kernel, out_shape=(jax.ShapeDtypeStruct((P_DEV, NT, ORIENT...  50.5 us
    unnamed x15, local copies, waits for them, and re-layouts  5.72 us

profile of v2, /device:TPU:1, one launch (start us, length us, event | category | flops | bytes accessed | tf_op | source)
XLA Modules:
  0.0 57.8 jit_solution(1282799237390358253)
XLA Ops:
  0.6 0.0 copy-start.5
  0.6 0.0 copy-start.6
  0.7 0.0 copy-start.4
  0.7 0.6 %copy-done.5 = s32[32]{0:T(128)S(1)} copy-done((s32[32]{0:T(128)S(1)}, s32[32]{0:T(128)}, u32[]{:S(2)}) %copy-start.5) | copy-done | bytes 152
  1.3 0.0 copy-done.6
  1.3 0.0 copy-done.4
  1.3 0.0 copy-start
  1.3 1.2 %copy-done = bf16[1024,2,256]{2,1,0:T(2,128)(2,1)S(1)} copy-done((bf16[1024,2,256]{2,1,0:T(2,128)(2,1)S(1)}, bf16[1024,2,256]{2,1,0:T(2,128)(2,1)}, u32[]{:S(2)}) %copy-start) | copy-done | bytes 1048600
  2.5 0.0 copy-start.1
  2.5 1.2 %copy-done.1 = bf16[4,256,2,256]{3,2,1,0:T(2,128)(2,1)S(1)} copy-done((bf16[4,256,2,256]{3,2,1,0:T(2,128)(2,1)S(1)}, bf16[4,256,2,256]{3,2,1,0:T(2,128)(2,1)}, u32[]{:S(2)}) %copy-start.1) | copy-done | bytes 1048600
  3.8 0.0 copy-start.2
  3.8 0.9 %copy-done.2 = f32[4,4,32,32]{3,2,1,0:T(8,128)S(1)} copy-done((f32[4,4,32,32]{3,2,1,0:T(8,128)S(1)}, f32[4,4,32,32]{3,2,1,0:T(8,128)}, u32[]{:S(2)}) %copy-start.2) | copy-done | bytes 65560
  4.7 0.0 copy-start.3
  4.7 0.7 %copy-done.3 = s32[4,256]{1,0:T(4,128)S(1)} copy-done((s32[4,256]{1,0:T(4,128)S(1)}, s32[4,256]{1,0:T(4,128)}, u32[]{:S(2)}) %copy-start.3) | copy-done | bytes 4120
  5.4 50.5 %cryo.1 = (f32[4,32,128]{2,1,0:T(8,128)S(1)}, bf16[1024,2,256]{2,1,0:T(2,128)(2,1)S(1)}) custom-call(s32[4,256]{1,0:T(4,128)S(1)} %copy-done.3, f32[512,32]{1,0:T(8,128)S(1)} %bitcast.4, f32[4]{0:T(128)S(1)} %copy-done.4, s32[32]{0:T(128)S(1)} %copy-done.5, s32[32]{0:T(128)S(1)} %copy-done.6, bf16[1024,2,256]{2,1,0:T(2,128)(2,1)S(1)} %copy-done, ...), custom_call_target="tpu_custom_call" | custom-call | tf_op jit(solution)/shard_map/cryo/pallas_call | solution.py:524
  55.9 0.2 reshape.11
  56.1 0.7 %copy.11 = f32[4,32,4,32]{3,1,2,0:T(8,128)} copy(f32[4,32,4,32]{3,2,1,0:T(4,128)S(1)} %reshape.11) | data formatting | bytes 131072 | tf_op jit(solution)/shard_map/reshape | solution.py:597
  56.8 1.0 %copy.13 = bf16[1024,2,256]{2,1,0:T(2,128)(2,1)} copy(bf16[1024,2,256]{2,1,0:T(2,128)(2,1)S(1)} %get-tuple-element.9) | data formatting | bytes 2097152
Async XLA Ops:
  0.6 0.7 %copy-start.5 = (s32[32]{0:T(128)S(1)}, s32[32]{0:T(128)}, u32[]{:S(2)}) copy-start(s32[32]{0:T(128)} %sy_hbm.1) | copy-start | bytes 388
  0.6 0.7 %copy-start.6 = (s32[32]{0:T(128)S(1)}, s32[32]{0:T(128)}, u32[]{:S(2)}) copy-start(s32[32]{0:T(128)} %sx_hbm.1) | copy-start | bytes 388
  0.7 0.7 %copy-start.4 = (f32[4]{0:T(128)S(1)}, f32[4]{0:T(128)}, u32[]{:S(2)}) copy-start(f32[4]{0:T(128)} %defocus_hbm.1) | copy-start | bytes 52
  1.3 1.2 %copy-start = (bf16[1024,2,256]{2,1,0:T(2,128)(2,1)S(1)}, bf16[1024,2,256]{2,1,0:T(2,128)(2,1)}, u32[]{:S(2)}) copy-start(bf16[1024,2,256]{2,1,0:T(2,128)(2,1)} %volume_hbm.1) | copy-start | bytes 3145732
  2.5 1.2 %copy-start.1 = (bf16[4,256,2,256]{3,2,1,0:T(2,128)(2,1)S(1)}, bf16[4,256,2,256]{3,2,1,0:T(2,128)(2,1)}, u32[]{:S(2)}) copy-start(bf16[4,256,2,256]{3,2,1,0:T(2,128)(2,1)} %images_hbm.1) | copy-start | bytes 3145732
  3.8 0.9 %copy-start.2 = (f32[4,4,32,32]{3,2,1,0:T(8,128)S(1)}, f32[4,4,32,32]{3,2,1,0:T(8,128)}, u32[]{:S(2)}) copy-start(f32[4,4,32,32]{3,2,1,0:T(8,128)} %param.10) | copy-start | bytes 196612
  4.7 0.7 %copy-start.3 = (s32[4,256]{1,0:T(4,128)S(1)}, s32[4,256]{1,0:T(4,128)}, u32[]{:S(2)}) copy-start(s32[4,256]{1,0:T(4,128)} %lines_hbm.1) | copy-start | bytes 12292

commit v3 on v2

--- a/solution.py
+++ b/solution.py
@@ -74,10 +74,10 @@
     scores_ref, update_hbm,
     lines_ref, weights_ref, defocus_ref, sy_ref, sx_ref,
     vbuf, ibuf, split, own, arrived, gather, insert, place_s, place_t,
-    fx, ephase, fy, hs, cx, term, sent, landed, xsend, xrecv, zsend, zrecv, ysend, yrecv,
-    agsend, agrecv, tile_z, tile_f32, rows, zacc, su,
+    fx, ephase, fy, hs, cx, term, sent, landed, xsend, xrecv, ysend, yrecv, zsend, zrecv,
+    fin, tile_y, rows, zacc, su,
     small_sem, in_sem, out_sem, s_send, s_recv, p_send, p_recv, x_send, x_recv, z_send, z_recv,
-    y_send, y_recv, a_send, a_recv,
+    y_send, y_recv, f_send, f_recv,
 ):
     dom = lax.axis_index("dom")
     slab = lax.axis_index("slab")
@@ -126,26 +126,30 @@
         return (to % 2) * 16 + zc, y * 2 + to // 2
 
     def y_peer(k):
-        to = lax.rem(x_lo * YS + y + k, XLO * YS)
-        return (to // YS) * 16 + zc, (to % YS) * 2 + x_hi
-
-    def dom_peer(k):
-        return x_lo * 16 + lax.rem(zc + k, 16), slab
+        return dom, lax.rem(y + k, YS) * 2 + x_hi
+
+    def z_peer(k):
+        return x_lo * 16 + lax.rem(z + k, ZS) * 2 + c, slab
+
+    def group_peer(k):
+        to = lax.rem(x_lo * 2 + c + k, 4)
+        return (to // 2) * 16 + z * 2 + to % 2, slab
 
     def greet(peer):
         pl.semaphore_signal(barrier, inc=1, device_id=peer, device_id_type=MESH)
 
-    def greet_both(k, carry):
+    def greet_slab(k, carry):
         greet(slab_peer(k))
-        greet(dom_peer(k))
         return carry
 
-    def greet_other(k, carry):
-        greet(((1 - x_lo) * 16 + zc, k * 2 + x_hi))
+    def greet_z(k, carry):
+        greet(z_peer(k))
         return carry
 
-    lax.fori_loop(1, SLABS, greet_both, 0)
-    lax.fori_loop(0, YS, greet_other, 0)
+    lax.fori_loop(1, SLABS, greet_slab, 0)
+    lax.fori_loop(1, ZS, greet_z, 0)
+    for k in range(1, 4):
+        greet(group_peer(k))
     greet(((1 - x_lo) * 16 + zc, y * 2 + 1 - x_hi))
 
     small[0].wait()
@@ -181,7 +185,7 @@
             at = slice(part * KS + j * 128, part * KS + j * 128 + 128)
             own[:, at] = picked[part * 32 : part * 32 + 32]
 
-    pl.semaphore_wait(barrier, 2 * (SLABS - 1) + YS + 1)
+    pl.semaphore_wait(barrier, SLABS - 1 + ZS - 1 + 3 + 1)
 
     def slab_copy(k):
         return pltpu.make_async_remote_copy(
@@ -230,7 +234,7 @@
     for o in range(ORIENT):
         rank = ranks[o]
         row = owner[o : o + 1]
-        at_t = (row & 1) * 128 + (rank >> 3) * 64 + (rank & 7) * YS + (row >> 1)
+        at_t = (row & 1) * 128 + (rank >> 3) * 64 + (row >> 1) * 8 + (rank & 7)
         place_t[o] = (iota((KS, KS), 0) == at_t).astype(F32).astype(BF16)
 
     freq_row = (iota((8, KS), 1) - HALF).astype(F32)
@@ -298,14 +302,23 @@
             device_id_type=MESH,
         )
 
-    def z_copy(j, k):
-        to = lax.rem(z + k, ZS)
+    def y_copy(j, k):
         return pltpu.make_async_remote_copy(
-            src_ref=zsend.at[j, to],
-            dst_ref=zrecv.at[j, z],
+            src_ref=ysend.at[j, lax.rem(y + k, YS)],
+            dst_ref=yrecv.at[j, y],
+            send_sem=y_send.at[0],
+            recv_sem=y_recv.at[0],
+            device_id=y_peer(k),
+            device_id_type=MESH,
+        )
+
+    def z_copy(k):
+        return pltpu.make_async_remote_copy(
+            src_ref=zsend,
+            dst_ref=zrecv.at[z],
             send_sem=z_send.at[0],
             recv_sem=z_recv.at[0],
-            device_id=(x_lo * 16 + to * 2 + c, slab),
+            device_id=z_peer(k),
             device_id_type=MESH,
         )
 
@@ -332,18 +345,6 @@
 
     lax.fori_loop(0, 2, keep, 0)
 
-    pltpu.make_async_copy(
-        arrived.at[0, pl.ds(0, SLABS - 1)], arrived.at[0, pl.ds(0, SLABS - 1)], s_recv.at[0]
-    ).wait()
-    forward = pltpu.make_async_remote_copy(
-        src_ref=arrived.at[c],
-        dst_ref=arrived.at[c],
-        send_sem=s_send.at[1],
-        recv_sem=s_recv.at[1],
-        device_id=partner,
-        device_id_type=MESH,
-    )
-    forward.start()
     for o in range(ORIENT):
         at_s = owner[o : o + 1] * OWNED + ranks[o]
         place_s[o] = (iota((KS, KS), 0) == at_s).astype(F32).astype(BF16)
@@ -380,8 +381,9 @@
                     else:
                         zacc[p, at] += part
 
-    correlate(c, True)
-
+    line_row = jnp.concatenate([2 * own_line, 2 * own_line + 1], 0).astype(F32)
+    line_row = jnp.broadcast_to(line_row, (128, 128)).T[0:1].astype(jnp.int32)
+    insert[...] = (iota((2 * LINES, 128), 0) == line_row).astype(F32).astype(BF16)
     def pass_on(j, carry):
         pltpu.make_async_copy(
             xrecv.at[j, pl.ds(0, 3)], xrecv.at[j, pl.ds(0, 3)], x_recv.at[j]
@@ -391,51 +393,69 @@
             total = xrecv[j, 0, :, at].astype(F32)
             for other in range(1, 4):
                 total += xrecv[j, other, :, at].astype(F32)
-            tile_z[:, part * YS : part * YS + YS] = total.reshape(ZS, YS, KS)
-        zsend[j] = tile_z[...].astype(BF16)
-
-        def send_z(k, inner):
-            z_copy(j, k).start()
+            tile_y[:, part * 8 : part * 8 + 8] = total.reshape(YS, 8, KS)
+        ysend[j] = tile_y[...].astype(BF16)
+
+        def send_y(k, inner):
+            y_copy(j, k).start()
             return inner
 
-        lax.fori_loop(1, ZS, send_z, 0)
-        zrecv[j, z] = zsend[j, z]
+        lax.fori_loop(1, YS, send_y, 0)
+        yrecv[j, y] = ysend[j, y]
         return carry
 
     lax.fori_loop(0, 2, pass_on, 0)
+    pltpu.make_async_copy(
+        arrived.at[0, pl.ds(0, SLABS - 1)], arrived.at[0, pl.ds(0, SLABS - 1)], s_recv.at[0]
+    ).wait()
+    forward = pltpu.make_async_remote_copy(
+        src_ref=arrived.at[c],
+        dst_ref=arrived.at[c],
+        send_sem=s_send.at[1],
+        recv_sem=s_recv.at[1],
+        device_id=partner,
+        device_id_type=MESH,
+    )
+    forward.start()
+    correlate(c, True)
+
+    pltpu.make_async_copy(
+        yrecv.at[:, pl.ds(0, YS - 1)], yrecv.at[:, pl.ds(0, YS - 1)], y_recv.at[0]
+    ).wait()
+    for j in range(2):
+        total = yrecv[j, 0].astype(F32)
+        for other in range(1, YS):
+            total += yrecv[j, other].astype(F32)
+        zsend[j] = total.astype(BF16)
+
+    def send_z(k, carry):
+        z_copy(k).start()
+        return carry
+
+    lax.fori_loop(1, ZS, send_z, 0)
+    zrecv[z] = zsend[...]
     forward.wait_recv()
     correlate(1 - c, False)
-    pltpu.make_async_copy(
-        zrecv.at[:, pl.ds(0, ZS - 1)], zrecv.at[:, pl.ds(0, ZS - 1)], z_recv.at[0]
-    ).wait()
-    for j in range(2):
-        total = zrecv[j, 0].astype(F32)
-        for other in range(1, ZS):
-            total += zrecv[j, other].astype(F32)
-        for part in range(2):
-            for b in range(2):
-                tile_f32[pl.ds(j * 4 + part * 2 + b, YS, stride=8), :] = total[
-                    part * YS : part * YS + YS, b * 128 : b * 128 + 128
-                ]
-    ysend[...] = tile_f32[0 : YS * 8].reshape(YS, 8, 128)
-
-    def y_copy(k):
-        to = lax.rem(x_lo * YS + y + k, XLO * YS)
+
+    pltpu.make_async_copy(zrecv.at[pl.ds(0, ZS - 1)], zrecv.at[pl.ds(0, ZS - 1)], z_recv.at[0]).wait()
+    total = zrecv[0].astype(F32)
+    for other in range(1, ZS):
+        total += zrecv[other].astype(F32)
+    place = x_lo * 2 + c
+    fin[place] = (total * SCALE).astype(BF16)
+
+    def group_copy(k):
         return pltpu.make_async_remote_copy(
-            src_ref=ysend.at[to % YS],
-            dst_ref=yrecv.at[x_lo * YS + y],
-            send_sem=y_send.at[0],
-            recv_sem=y_recv.at[0],
-            device_id=y_peer(k),
+            src_ref=fin.at[place],
+            dst_ref=fin.at[place],
+            send_sem=f_send.at[0],
+            recv_sem=f_recv.at[0],
+            device_id=group_peer(k),
             device_id_type=MESH,
         )
 
-    def send_y(k, carry):
-        y_copy(k).start()
-        return carry
-
-    lax.fori_loop(1, XLO * YS, send_y, 0)
-    yrecv[x_lo * YS + y] = ysend[y]
+    for k in range(1, 4):
+        group_copy(k).start()
     for p in range(P_DEV):
         full = jnp.concatenate([zacc[p, :, 0:128], zacc[p, :, 128:]], 0)
         full_hi = full.astype(BF16)
@@ -443,47 +463,14 @@
         both = dot(fy[...], full_hi)
         scores_ref[p] = both[0:NT] + both[NT:] + dot(fy[0:NT], full_lo)
 
-    line_row = jnp.concatenate([2 * own_line, 2 * own_line + 1], 0).astype(F32)
-    line_row = jnp.broadcast_to(line_row, (128, 128)).T[0:1].astype(jnp.int32)
-    insert[...] = (iota((2 * LINES, 128), 0) == line_row).astype(F32).astype(BF16)
-    pltpu.make_async_copy(
-        yrecv.at[pl.ds(0, XLO * YS - 1)], yrecv.at[pl.ds(0, XLO * YS - 1)], y_recv.at[0]
-    ).wait()
-    sums = []
-    for half in range(XLO):
-        total = yrecv[half * YS]
-        for other in range(1, YS):
-            total += yrecv[half * YS + other]
-        sums.append(total * SCALE)
-    agsend[...] = jnp.concatenate(sums, 0).astype(BF16)
-
-    def dom_copy(k):
-        return pltpu.make_async_remote_copy(
-            src_ref=agsend,
-            dst_ref=agrecv.at[zc],
-            send_sem=a_send.at[0],
-            recv_sem=a_recv.at[0],
-            device_id=dom_peer(k),
-            device_id_type=MESH,
-        )
-
-    def send_dom(k, carry):
-        dom_copy(k).start()
-        return carry
-
-    lax.fori_loop(1, 16, send_dom, 0)
-    agrecv[zc] = agsend[...]
-    pltpu.make_async_copy(agrecv.at[pl.ds(0, 15)], agrecv.at[pl.ds(0, 15)], a_recv.at[0]).wait()
-
-    tile_f32[...] = agrecv[...].astype(F32).reshape(256, 128)
+    pltpu.make_async_copy(fin.at[pl.ds(0, 3)], fin.at[pl.ds(0, 3)], f_recv.at[0]).wait()
+
     for o in range(ORIENT):
         for r in range(2):
-            for b in range(4):
-                got = tile_f32[
-                    pl.ds((o // 2) * 16 + r * 8 + (o % 2) * 4 + b, ZS, stride=32), :
-                ]
-                first = (b // 2) * 64 + o * OWNED + r * 8
-                rows[first : first + 8, (b % 2) * 128 : (b % 2) * 128 + 128] = got
+            got = fin[r * 2 + o // 2, o % 2].astype(F32)
+            for part in range(2):
+                first = part * 64 + o * OWNED + r * 8
+                rows[first : first + 8] = got[part * 8 : part * 8 + 8]
     rows_bf16 = rows[...].astype(BF16)
     placed = dot(insert[...], rows_bf16).astype(BF16)
     outs = []
@@ -507,19 +494,17 @@
             xrecv.at[j, pl.ds(0, 3)], xrecv.at[j, pl.ds(0, 3)], x_send.at[j]
         ).wait()
     pltpu.make_async_copy(
-        zrecv.at[:, pl.ds(0, ZS - 1)], zrecv.at[:, pl.ds(0, ZS - 1)], z_send.at[0]
+        yrecv.at[:, pl.ds(0, YS - 1)], yrecv.at[:, pl.ds(0, YS - 1)], y_send.at[0]
     ).wait()
-    pltpu.make_async_copy(
-        yrecv.at[pl.ds(0, XLO * YS - 1)], yrecv.at[pl.ds(0, XLO * YS - 1)], y_send.at[0]
-    ).wait()
-    pltpu.make_async_copy(agrecv.at[pl.ds(0, 15)], agrecv.at[pl.ds(0, 15)], a_send.at[0]).wait()
+    pltpu.make_async_copy(zrecv.at[pl.ds(0, ZS - 1)], zrecv.at[pl.ds(0, ZS - 1)], z_send.at[0]).wait()
+    pltpu.make_async_copy(fin.at[pl.ds(0, 3)], fin.at[pl.ds(0, 3)], f_send.at[0]).wait()
     for out in outs:
         out.wait()
 
 
 def body(volume, images, defocus, soft_weights, slice_lines, shift_y, shift_x):
     vmem = pl.BlockSpec(memory_space=pltpu.VMEM)
-    hbm = pl.BlockSpec(memory_space=pl.ANY)
+    hbm = pl.BlockSpec(memory_space=pltpu.HBM)
     dma = pltpu.SemaphoreType.DMA
     scores, line_update = pl.pallas_call(
         kernel,
@@ -554,14 +539,12 @@
             pltpu.VMEM((2, KS, 2 * KS), BF16),
             pltpu.VMEM((2, 4, 64, 2 * KS), BF16),
             pltpu.VMEM((2, 4, 64, 2 * KS), BF16),
-            pltpu.VMEM((2, ZS, 16, KS), BF16),
-            pltpu.VMEM((2, ZS, 16, KS), BF16),
-            pltpu.VMEM((YS, 8, 128), F32),
-            pltpu.VMEM((XLO * YS, 8, 128), F32),
-            pltpu.VMEM((16, 128), BF16),
-            pltpu.VMEM((16, 16, 128), BF16),
-            pltpu.VMEM((ZS, 16, KS), F32),
-            pltpu.VMEM((256, 128), F32),
+            pltpu.VMEM((2, YS, 16, KS), BF16),
+            pltpu.VMEM((2, YS, 16, KS), BF16),
+            pltpu.VMEM((2, 16, KS), BF16),
+            pltpu.VMEM((ZS, 2, 16, KS), BF16),
+            pltpu.VMEM((4, 2, 16, KS), BF16),
+            pltpu.VMEM((YS, 16, KS), F32),
             pltpu.VMEM((2 * ORIENT * OWNED, KS), F32),
             pltpu.VMEM((P_DEV, KS, 256), F32),
             pltpu.VMEM((KS, 2 * KS), F32),

time: 58.1 us -> 54.5 us (0.938)
  Pallas kernels: 50.5 us -> 46.9 us
    pallas_call x1, Pallas kernels: 50.5 us -> 46.9 us  [body(): pl.pallas_call(kernel, out_shape=(jax.ShapeDtypeStruct((P_DEV, NT, ORIENT...]
where the time goes in v3:
time: 54.5 us; the launch traced here: 54.2 us
  Pallas kernels  46.9 us (86%)
  local copies, waits for them, and re-layouts  6.61 us (12%)
  between operations  0.68 us (1%)
    pallas_call x1, Pallas kernels, body(): pl.pallas_call(kernel, out_shape=(jax.ShapeDtypeStruct((P_DEV, NT, ORIENT...  46.9 us
    unnamed x15, local copies, waits for them, and re-layouts  5.72 us

profile of v3, /device:TPU:1, one launch (start us, length us, event | category | flops | bytes accessed | tf_op | source)
XLA Modules:
  0.0 54.2 jit_solution(5362024706759863444)
XLA Ops:
  0.6 0.0 copy-start.5
  0.6 0.0 copy-start.6
  0.7 0.0 copy-start.4
  0.7 0.6 %copy-done.5 = s32[32]{0:T(128)S(1)} copy-done((s32[32]{0:T(128)S(1)}, s32[32]{0:T(128)}, u32[]{:S(2)}) %copy-start.5) | copy-done | bytes 152
  1.3 0.0 copy-done.6
  1.3 0.0 copy-done.4
  1.3 0.0 copy-start
  1.3 1.2 %copy-done = bf16[1024,2,256]{2,1,0:T(2,128)(2,1)S(1)} copy-done((bf16[1024,2,256]{2,1,0:T(2,128)(2,1)S(1)}, bf16[1024,2,256]{2,1,0:T(2,128)(2,1)}, u32[]{:S(2)}) %copy-start) | copy-done | bytes 1048600
  2.5 0.0 copy-start.1
  2.5 1.2 %copy-done.1 = bf16[4,256,2,256]{3,2,1,0:T(2,128)(2,1)S(1)} copy-done((bf16[4,256,2,256]{3,2,1,0:T(2,128)(2,1)S(1)}, bf16[4,256,2,256]{3,2,1,0:T(2,128)(2,1)}, u32[]{:S(2)}) %copy-start.1) | copy-done | bytes 1048600
  3.8 0.0 copy-start.2
  3.8 0.9 %copy-done.2 = f32[4,4,32,32]{3,2,1,0:T(8,128)S(1)} copy-done((f32[4,4,32,32]{3,2,1,0:T(8,128)S(1)}, f32[4,4,32,32]{3,2,1,0:T(8,128)}, u32[]{:S(2)}) %copy-start.2) | copy-done | bytes 65560
  4.7 0.0 copy-start.3
  4.7 0.7 %copy-done.3 = s32[4,256]{1,0:T(4,128)S(1)} copy-done((s32[4,256]{1,0:T(4,128)S(1)}, s32[4,256]{1,0:T(4,128)}, u32[]{:S(2)}) %copy-start.3) | copy-done | bytes 4120
  5.4 46.9 %cryo.1 = (f32[4,32,128]{2,1,0:T(8,128)S(1)}, bf16[1024,2,256]{2,1,0:T(2,128)(2,1)S(1)}) custom-call(s32[4,256]{1,0:T(4,128)S(1)} %copy-done.3, f32[512,32]{1,0:T(8,128)S(1)} %bitcast.4, f32[4]{0:T(128)S(1)} %copy-done.4, s32[32]{0:T(128)S(1)} %copy-done.5, s32[32]{0:T(128)S(1)} %copy-done.6, bf16[1024,2,256]{2,1,0:T(2,128)(2,1)S(1)} %copy-done, ...), custom_call_target="tpu_custom_call" | custom-call | tf_op jit(solution)/shard_map/cryo/pallas_call | solution.py:509
  52.3 0.2 reshape.11
  52.5 0.7 %copy.11 = f32[4,32,4,32]{3,1,2,0:T(8,128)} copy(f32[4,32,4,32]{3,2,1,0:T(4,128)S(1)} %reshape.11) | data formatting | bytes 131072 | tf_op jit(solution)/shard_map/reshape | solution.py:580
  53.2 1.0 %copy.13 = bf16[1024,2,256]{2,1,0:T(2,128)(2,1)} copy(bf16[1024,2,256]{2,1,0:T(2,128)(2,1)S(1)} %get-tuple-element.9) | data formatting | bytes 2097152
Async XLA Ops:
  0.6 0.7 %copy-start.5 = (s32[32]{0:T(128)S(1)}, s32[32]{0:T(128)}, u32[]{:S(2)}) copy-start(s32[32]{0:T(128)} %sy_hbm.1) | copy-start | bytes 388
  0.6 0.7 %copy-start.6 = (s32[32]{0:T(128)S(1)}, s32[32]{0:T(128)}, u32[]{:S(2)}) copy-start(s32[32]{0:T(128)} %sx_hbm.1) | copy-start | bytes 388
  0.7 0.7 %copy-start.4 = (f32[4]{0:T(128)S(1)}, f32[4]{0:T(128)}, u32[]{:S(2)}) copy-start(f32[4]{0:T(128)} %defocus_hbm.1) | copy-start | bytes 52
  1.3 1.2 %copy-start = (bf16[1024,2,256]{2,1,0:T(2,128)(2,1)S(1)}, bf16[1024,2,256]{2,1,0:T(2,128)(2,1)}, u32[]{:S(2)}) copy-start(bf16[1024,2,256]{2,1,0:T(2,128)(2,1)} %volume_hbm.1) | copy-start | bytes 3145732
  2.5 1.2 %copy-start.1 = (bf16[4,256,2,256]{3,2,1,0:T(2,128)(2,1)S(1)}, bf16[4,256,2,256]{3,2,1,0:T(2,128)(2,1)}, u32[]{:S(2)}) copy-start(bf16[4,256,2,256]{3,2,1,0:T(2,128)(2,1)} %images_hbm.1) | copy-start | bytes 3145732
  3.8 0.9 %copy-start.2 = (f32[4,4,32,32]{3,2,1,0:T(8,128)S(1)}, f32[4,4,32,32]{3,2,1,0:T(8,128)}, u32[]{:S(2)}) copy-start(f32[4,4,32,32]{3,2,1,0:T(8,128)} %param.10) | copy-start | bytes 196612
  4.7 0.7 %copy-start.3 = (s32[4,256]{1,0:T(4,128)S(1)}, s32[4,256]{1,0:T(4,128)}, u32[]{:S(2)}) copy-start(s32[4,256]{1,0:T(4,128)} %lines_hbm.1) | copy-start | bytes 12292

commit v4 on v3

--- a/solution.py
+++ b/solution.py
@@ -119,7 +119,9 @@
     barrier = pltpu.get_barrier_semaphore()
 
     def slab_peer(k):
-        return dom, lax.rem(slab + k, SLABS)
+        to = lax.rem(slab + k, SLABS)
+        flip = (to % 2 + x_hi) % 2
+        return ((x_lo + flip) % 2) * 16 + zc, to
 
     def x_peer(k):
         to = lax.rem(x + k, 4)
@@ -150,7 +152,7 @@
     lax.fori_loop(1, ZS, greet_z, 0)
     for k in range(1, 4):
         greet(group_peer(k))
-    greet(((1 - x_lo) * 16 + zc, y * 2 + 1 - x_hi))
+    greet((dom, y * 2 + 1 - x_hi))
 
     small[0].wait()
     lines = lines_ref[...]
@@ -352,10 +354,11 @@
     for o in range(ORIENT):
         cos_o = jnp.where(group == o, cos_x, 0.0).astype(BF16)
         sin_o = jnp.where(group == o, sin_x, 0.0).astype(BF16)
-        fx[o, 0:KS, 0:128] = cos_o
-        fx[o, 0:KS, 128:] = -sin_o
-        fx[o, KS:, 0:128] = sin_o
-        fx[o, KS:, 128:] = cos_o
+        at = (o % 2) * 2 * KS
+        fx[o // 2, at : at + KS, 0:128] = cos_o
+        fx[o // 2, at : at + KS, 128:] = -sin_o
+        fx[o // 2, at + KS : at + 2 * KS, 0:128] = sin_o
+        fx[o // 2, at + KS : at + 2 * KS, 128:] = cos_o
     table_y = jnp.concatenate([cos_y.T[0:NT], sin_y.T[0:NT]], 1) * (1.0 / KS)
     fy_hi = table_y.astype(BF16)
     fy[0:NT] = fy_hi
@@ -363,23 +366,24 @@
 
     def correlate(half, first):
         for j in range(2):
-            o = 2 * half + j
             rows_s = arrived[half, :, j * OWNED : (j + 1) * OWNED, :].reshape(KS, 2 * KS)
-            su[...] = dot_t(place_s[o], rows_s)
-            for block in range(2):
-                at = slice(block * 128, block * 128 + 128)
-                for p in range(P_DEV):
-                    s_re = su[at, 0:KS]
-                    s_im = su[at, KS:]
-                    c_re = cx[p, 0, at]
-                    c_im = cx[p, 1, at]
-                    q_re = (s_re * c_re + s_im * c_im).astype(BF16)
-                    q_im = (s_re * c_im - s_im * c_re).astype(BF16)
-                    part = dot(q_re, fx[o, 0:KS]) + dot(q_im, fx[o, KS:])
-                    if first and j == 0:
-                        zacc[p, at] = part
-                    else:
-                        zacc[p, at] += part
+            su[j] = dot_t(place_s[2 * half + j], rows_s)
+        for block in range(2):
+            at = slice(block * 128, block * 128 + 128)
+            for p in range(P_DEV):
+                c_re = cx[p, 0, at]
+                c_im = cx[p, 1, at]
+                q = []
+                for j in range(2):
+                    s_re = su[j, at, 0:KS]
+                    s_im = su[j, at, KS:]
+                    q.append((s_re * c_re + s_im * c_im).astype(BF16))
+                    q.append((s_re * c_im - s_im * c_re).astype(BF16))
+                part = dot(jnp.concatenate(q, 1), fx[half])
+                if first:
+                    zacc[p, at] = part
+                else:
+                    zacc[p, at] += part
 
     line_row = jnp.concatenate([2 * own_line, 2 * own_line + 1], 0).astype(F32)
     line_row = jnp.broadcast_to(line_row, (128, 128)).T[0:1].astype(jnp.int32)
@@ -472,16 +476,21 @@
                 first = part * 64 + o * OWNED + r * 8
                 rows[first : first + 8] = got[part * 8 : part * 8 + 8]
     rows_bf16 = rows[...].astype(BF16)
-    placed = dot(insert[...], rows_bf16).astype(BF16)
     outs = []
-    for j in range(2):
-        vbuf.at[j].reshape(2 * LINES, 128)[...] = placed[:, j * 128 : j * 128 + 128]
-        outs.append(
-            pltpu.make_async_copy(
-                vbuf.at[j], update_hbm.at[:, :, pl.ds(j * 128, 128)], out_sem.at[j]
+    for piece in range(4):
+        at = slice(piece * 512, piece * 512 + 512)
+        of = pl.ds(piece * 256, 256)
+        placed = dot(insert[at], rows_bf16).astype(BF16)
+        for j in range(2):
+            vbuf.at[j, of].reshape(512, 128)[...] = placed[:, j * 128 : j * 128 + 128]
+            outs.append(
+                pltpu.make_async_copy(
+                    vbuf.at[j, of],
+                    update_hbm.at[of, :, pl.ds(j * 128, 128)],
+                    out_sem.at[piece * 2 + j],
+                )
             )
-        )
-        outs[j].start()
+            outs[-1].start()
 
     pltpu.make_async_copy(
         arrived.at[0, pl.ds(0, SLABS - 1)], arrived.at[0, pl.ds(0, SLABS - 1)], s_send.at[0]
@@ -529,7 +538,7 @@
             pltpu.VMEM((2 * LINES, 2 * ORIENT * OWNED), BF16),
             pltpu.VMEM((ORIENT, KS, KS), BF16),
             pltpu.VMEM((ORIENT, KS, KS), BF16),
-            pltpu.VMEM((ORIENT, 2 * KS, 256), BF16),
+            pltpu.VMEM((2, 4 * KS, 256), BF16),
             pltpu.VMEM((2 * KS, 2 * NT), BF16),
             pltpu.VMEM((2 * NT, 2 * KS), BF16),
             pltpu.VMEM((P_DEV * ORIENT, 2 * NT, KS), BF16),
@@ -547,10 +556,10 @@
             pltpu.VMEM((YS, 16, KS), F32),
             pltpu.VMEM((2 * ORIENT * OWNED, KS), F32),
             pltpu.VMEM((P_DEV, KS, 256), F32),
-            pltpu.VMEM((KS, 2 * KS), F32),
+            pltpu.VMEM((2, KS, 2 * KS), F32),
             dma((5,)),
             dma((4,)),
-            dma((2,)),
+            dma((8,)),
             dma((2,)),
             dma((2,)),
             dma((2,)),
@@ -565,7 +574,7 @@
             dma((1,)),
         ],
         compiler_params=pltpu.CompilerParams(
-            collective_id=0, has_side_effects=True, vmem_limit_bytes=48 * 1024 * 1024
+            collective_id=0, has_side_effects=True, vmem_limit_bytes=60 * 1024 * 1024
         ),
         name="cryo",
     )(

time: 54.5 us -> 52.4 us (0.961)
  local copies, waits for them, and re-layouts: 6.61 us -> 4.65 us
    unnamed x15 -> x1, local copies, waits for them, and re-layouts: 5.72 us -> 2.91 us
    reshape x2, local copies, waits for them, and re-layouts: 0.9 us -> 1.73 us  [body(): scores = scores.reshape(P_DEV, NT, ORIENT, NT).transpose(0, 2, 1, 3)]
where the time goes in v4:
time: 52.4 us; the launch traced here: 52.2 us
  Pallas kernels  46.9 us (90%)
  local copies, waits for them, and re-layouts  4.65 us (9%)
  between operations  0.65 us (1%)
    pallas_call x1, Pallas kernels, body(): pl.pallas_call(kernel, out_shape=(jax.ShapeDtypeStruct((P_DEV, NT, ORIENT...  46.9 us
    unnamed x1, local copies, waits for them, and re-layouts  2.91 us
    reshape x2, local copies, waits for them, and re-layouts, body(): scores = scores.reshape(P_DEV, NT, ORIENT, NT).transpose(0, 2, 1, 3)  1.73 us

profile of v4, /device:TPU:1, one launch (start us, length us, event | category | flops | bytes accessed | tf_op | source)
XLA Modules:
  0.0 52.2 jit_solution(107078107269821970)
XLA Ops:
  0.6 46.9 %cryo.1 = (f32[4,32,128]{2,1,0:T(8,128)}, bf16[1024,2,256]{2,1,0:T(2,128)(2,1)}) custom-call(s32[4,256]{1,0:T(4,128)} %lines_hbm.1, f32[512,32]{1,0:T(8,128)} %bitcast.4, f32[4]{0:T(128)} %defocus_hbm.1, s32[32]{0:T(128)} %sy_hbm.1, s32[32]{0:T(128)} %sx_hbm.1, bf16[1024,2,256]{2,1,0:T(2,128)(2,1)} %volume_hbm.1, bf16[4,256,2,256]{3,2,1,0:T(2,128)(2,1)} %images_hbm.1), custom_call_target="tpu_custom_call" | custom-call | tf_op jit(solution)/shard_map/cryo/pallas_call | solution.py:518
  47.5 1.0 %reshape.11 = f32[4,32,4,32]{3,2,1,0:T(4,128)S(1)} reshape(f32[4,32,128]{2,1,0:T(8,128)} %get-tuple-element.4) | data formatting | bytes 131072 | tf_op jit(solution)/shard_map/reshape | solution.py:589
  48.5 0.7 %copy.11 = f32[4,32,4,32]{3,1,2,0:T(8,128)} copy(f32[4,32,4,32]{3,2,1,0:T(4,128)S(1)} %reshape.11) | data formatting | bytes 131072 | tf_op jit(solution)/shard_map/reshape | solution.py:589
  49.3 2.9 %copy.13 = bf16[1024,2,256]{2,1,0:T(2,128)(2,1)} copy(bf16[1024,2,256]{2,1,0:T(2,128)(2,1)} %get-tuple-element.9) | data formatting | bytes 2097152

commit v5 on v4

--- a/solution.py
+++ b/solution.py
@@ -71,11 +71,11 @@
 
 def kernel(
     lines_hbm, weights_hbm, defocus_hbm, sy_hbm, sx_hbm, volume_hbm, images_hbm,
-    scores_ref, update_hbm,
-    lines_ref, weights_ref, defocus_ref, sy_ref, sx_ref,
-    vbuf, ibuf, split, own, arrived, gather, insert, place_s, place_t,
+    scores_hbm, rows_hbm, line_hbm,
+    scores_ref, line_ref, lines_ref, weights_ref, defocus_ref, sy_ref, sx_ref,
+    vbuf, ibuf, split, own, arrived, gather, place_s, place_t,
     fx, ephase, fy, hs, cx, term, sent, landed, xsend, xrecv, ysend, yrecv, zsend, zrecv,
-    fin, tile_y, rows, zacc, su,
+    fin, tile_y, zacc, su,
     small_sem, in_sem, out_sem, s_send, s_recv, p_send, p_recv, x_send, x_recv, z_send, z_recv,
     y_send, y_recv, f_send, f_recv,
 ):
@@ -308,18 +308,18 @@
         return pltpu.make_async_remote_copy(
             src_ref=ysend.at[j, lax.rem(y + k, YS)],
             dst_ref=yrecv.at[j, y],
-            send_sem=y_send.at[0],
-            recv_sem=y_recv.at[0],
+            send_sem=y_send.at[j],
+            recv_sem=y_recv.at[j],
             device_id=y_peer(k),
             device_id_type=MESH,
         )
 
-    def z_copy(k):
+    def z_copy(j, k):
         return pltpu.make_async_remote_copy(
-            src_ref=zsend,
-            dst_ref=zrecv.at[z],
-            send_sem=z_send.at[0],
-            recv_sem=z_recv.at[0],
+            src_ref=zsend.at[j],
+            dst_ref=zrecv.at[j, z],
+            send_sem=z_send.at[j],
+            recv_sem=z_recv.at[j],
             device_id=z_peer(k),
             device_id_type=MESH,
         )
@@ -386,8 +386,10 @@
                     zacc[p, at] += part
 
     line_row = jnp.concatenate([2 * own_line, 2 * own_line + 1], 0).astype(F32)
-    line_row = jnp.broadcast_to(line_row, (128, 128)).T[0:1].astype(jnp.int32)
-    insert[...] = (iota((2 * LINES, 128), 0) == line_row).astype(F32).astype(BF16)
+    line_row = jnp.broadcast_to(line_row, (128, 128)).T[0:8].astype(jnp.int32)
+    line_ref[...] = line_row
+    outs = [pltpu.make_async_copy(line_ref, line_hbm, out_sem.at[0])]
+    outs[0].start()
     def pass_on(j, carry):
         pltpu.make_async_copy(
             xrecv.at[j, pl.ds(0, 3)], xrecv.at[j, pl.ds(0, 3)], x_recv.at[j]
@@ -423,30 +425,36 @@
     forward.start()
     correlate(c, True)
 
-    pltpu.make_async_copy(
-        yrecv.at[:, pl.ds(0, YS - 1)], yrecv.at[:, pl.ds(0, YS - 1)], y_recv.at[0]
-    ).wait()
-    for j in range(2):
+    def spread(j, carry):
+        pltpu.make_async_copy(
+            yrecv.at[j, pl.ds(0, YS - 1)], yrecv.at[j, pl.ds(0, YS - 1)], y_recv.at[j]
+        ).wait()
         total = yrecv[j, 0].astype(F32)
         for other in range(1, YS):
             total += yrecv[j, other].astype(F32)
         zsend[j] = total.astype(BF16)
 
-    def send_z(k, carry):
-        z_copy(k).start()
+        def send_z(k, inner):
+            z_copy(j, k).start()
+            return inner
+
+        lax.fori_loop(1, ZS, send_z, 0)
+        zrecv[j, z] = zsend[j]
         return carry
 
-    lax.fori_loop(1, ZS, send_z, 0)
-    zrecv[z] = zsend[...]
+    lax.fori_loop(0, 2, spread, 0)
     forward.wait_recv()
     correlate(1 - c, False)
 
-    pltpu.make_async_copy(zrecv.at[pl.ds(0, ZS - 1)], zrecv.at[pl.ds(0, ZS - 1)], z_recv.at[0]).wait()
-    total = zrecv[0].astype(F32)
-    for other in range(1, ZS):
-        total += zrecv[other].astype(F32)
     place = x_lo * 2 + c
-    fin[place] = (total * SCALE).astype(BF16)
+    for j in range(2):
+        pltpu.make_async_copy(
+            zrecv.at[j, pl.ds(0, ZS - 1)], zrecv.at[j, pl.ds(0, ZS - 1)], z_recv.at[j]
+        ).wait()
+        total = zrecv[j, 0].astype(F32)
+        for other in range(1, ZS):
+            total += zrecv[j, other].astype(F32)
+        fin[place, j] = (total * SCALE).astype(BF16)
 
     def group_copy(k):
         return pltpu.make_async_remote_copy(
@@ -466,31 +474,12 @@
         full_lo = (full - full_hi.astype(F32)).astype(BF16)
         both = dot(fy[...], full_hi)
         scores_ref[p] = both[0:NT] + both[NT:] + dot(fy[0:NT], full_lo)
+    outs.append(pltpu.make_async_copy(scores_ref, scores_hbm, out_sem.at[1]))
+    outs[1].start()
 
     pltpu.make_async_copy(fin.at[pl.ds(0, 3)], fin.at[pl.ds(0, 3)], f_recv.at[0]).wait()
-
-    for o in range(ORIENT):
-        for r in range(2):
-            got = fin[r * 2 + o // 2, o % 2].astype(F32)
-            for part in range(2):
-                first = part * 64 + o * OWNED + r * 8
-                rows[first : first + 8] = got[part * 8 : part * 8 + 8]
-    rows_bf16 = rows[...].astype(BF16)
-    outs = []
-    for piece in range(4):
-        at = slice(piece * 512, piece * 512 + 512)
-        of = pl.ds(piece * 256, 256)
-        placed = dot(insert[at], rows_bf16).astype(BF16)
-        for j in range(2):
-            vbuf.at[j, of].reshape(512, 128)[...] = placed[:, j * 128 : j * 128 + 128]
-            outs.append(
-                pltpu.make_async_copy(
-                    vbuf.at[j, of],
-                    update_hbm.at[of, :, pl.ds(j * 128, 128)],
-                    out_sem.at[piece * 2 + j],
-                )
-            )
-            outs[-1].start()
+    outs.append(pltpu.make_async_copy(fin, rows_hbm, out_sem.at[2]))
+    outs[2].start()
 
     pltpu.make_async_copy(
         arrived.at[0, pl.ds(0, SLABS - 1)], arrived.at[0, pl.ds(0, SLABS - 1)], s_send.at[0]
@@ -502,11 +491,43 @@
         pltpu.make_async_copy(
             xrecv.at[j, pl.ds(0, 3)], xrecv.at[j, pl.ds(0, 3)], x_send.at[j]
         ).wait()
-    pltpu.make_async_copy(
-        yrecv.at[:, pl.ds(0, YS - 1)], yrecv.at[:, pl.ds(0, YS - 1)], y_send.at[0]
-    ).wait()
-    pltpu.make_async_copy(zrecv.at[pl.ds(0, ZS - 1)], zrecv.at[pl.ds(0, ZS - 1)], z_send.at[0]).wait()
+    for j in range(2):
+        pltpu.make_async_copy(
+            yrecv.at[j, pl.ds(0, YS - 1)], yrecv.at[j, pl.ds(0, YS - 1)], y_send.at[j]
+        ).wait()
+        pltpu.make_async_copy(
+            zrecv.at[j, pl.ds(0, ZS - 1)], zrecv.at[j, pl.ds(0, ZS - 1)], z_send.at[j]
+        ).wait()
     pltpu.make_async_copy(fin.at[pl.ds(0, 3)], fin.at[pl.ds(0, 3)], f_send.at[0]).wait()
+    for out in outs:
+        out.wait()
+
+
+def finish(fin_ref, line_ref, found_ref, scores_ref, update_hbm, rows, buf, out_sem):
+    for o in range(ORIENT):
+        for r in range(2):
+            got = fin_ref[r * 2 + o // 2, o % 2].astype(F32)
+            for part in range(2):
+                first = part * 64 + o * OWNED + r * 8
+                rows[first : first + 8] = got[part * 8 : part * 8 + 8]
+    rows_bf16 = rows[...].astype(BF16)
+    outs = []
+    for piece in range(4):
+        of = pl.ds(piece * 256, 256)
+        insert = iota((512, 128), 0) + piece * 512 == line_ref[0:1]
+        placed = dot(insert.astype(F32).astype(BF16), rows_bf16).astype(BF16)
+        for j in range(2):
+            buf.at[j, of].reshape(512, 128)[...] = placed[:, j * 128 : j * 128 + 128]
+            outs.append(
+                pltpu.make_async_copy(
+                    buf.at[j, of],
+                    update_hbm.at[of, :, pl.ds(j * 128, 128)],
+                    out_sem.at[piece * 2 + j],
+                )
+            )
+            outs[-1].start()
+    for o in range(ORIENT):
+        scores_ref[:, o] = found_ref[:, :, o * NT : (o + 1) * NT]
     for out in outs:
         out.wait()
 
@@ -515,15 +536,18 @@
     vmem = pl.BlockSpec(memory_space=pltpu.VMEM)
     hbm = pl.BlockSpec(memory_space=pltpu.HBM)
     dma = pltpu.SemaphoreType.DMA
-    scores, line_update = pl.pallas_call(
+    found, rows, line = pl.pallas_call(
         kernel,
         out_shape=(
             jax.ShapeDtypeStruct((P_DEV, NT, ORIENT * NT), F32),
-            jax.ShapeDtypeStruct((LINES, 2, KS), BF16),
+            jax.ShapeDtypeStruct((4, 2, 16, KS), BF16),
+            jax.ShapeDtypeStruct((8, 128), jnp.int32),
         ),
         in_specs=[hbm] * 7,
-        out_specs=(vmem, hbm),
+        out_specs=(hbm, hbm, hbm),
         scratch_shapes=[
+            pltpu.VMEM((P_DEV, NT, ORIENT * NT), F32),
+            pltpu.VMEM((8, 128), jnp.int32),
             pltpu.VMEM((ORIENT, KS), jnp.int32),
             pltpu.VMEM((P_DEV * ORIENT * NT, NT), F32),
             pltpu.SMEM((P_DEV,), F32),
@@ -535,7 +559,6 @@
             pltpu.VMEM((2 * OWNED, 2 * KS), BF16),
             pltpu.VMEM((2, SLABS, 2 * OWNED, 2 * KS), BF16),
             pltpu.VMEM((4 * OWNED, 2 * LINES), BF16),
-            pltpu.VMEM((2 * LINES, 2 * ORIENT * OWNED), BF16),
             pltpu.VMEM((ORIENT, KS, KS), BF16),
             pltpu.VMEM((ORIENT, KS, KS), BF16),
             pltpu.VMEM((2, 4 * KS, 256), BF16),
@@ -551,25 +574,24 @@
             pltpu.VMEM((2, YS, 16, KS), BF16),
             pltpu.VMEM((2, YS, 16, KS), BF16),
             pltpu.VMEM((2, 16, KS), BF16),
-            pltpu.VMEM((ZS, 2, 16, KS), BF16),
+            pltpu.VMEM((2, ZS, 16, KS), BF16),
             pltpu.VMEM((4, 2, 16, KS), BF16),
             pltpu.VMEM((YS, 16, KS), F32),
-            pltpu.VMEM((2 * ORIENT * OWNED, KS), F32),
             pltpu.VMEM((P_DEV, KS, 256), F32),
             pltpu.VMEM((2, KS, 2 * KS), F32),
             dma((5,)),
             dma((4,)),
-            dma((8,)),
-            dma((2,)),
-            dma((2,)),
-            dma((2,)),
-            dma((2,)),
-            dma((2,)),
-            dma((2,)),
-            dma((1,)),
-            dma((1,)),
-            dma((1,)),
-            dma((1,)),
+            dma((3,)),
+            dma((2,)),
+            dma((2,)),
+            dma((2,)),
+            dma((2,)),
+            dma((2,)),
+            dma((2,)),
+            dma((2,)),
+            dma((2,)),
+            dma((2,)),
+            dma((2,)),
             dma((1,)),
             dma((1,)),
         ],
@@ -586,8 +608,22 @@
         volume,
         images,
     )
-    scores = scores.reshape(P_DEV, NT, ORIENT, NT).transpose(0, 2, 1, 3)
-    return scores, line_update
+    return pl.pallas_call(
+        finish,
+        out_shape=(
+            jax.ShapeDtypeStruct((P_DEV, ORIENT, NT, NT), F32),
+            jax.ShapeDtypeStruct((LINES, 2, KS), BF16),
+        ),
+        in_specs=[vmem] * 3,
+        out_specs=(vmem, hbm),
+        scratch_shapes=[
+            pltpu.VMEM((2 * ORIENT * OWNED, KS), F32),
+            pltpu.VMEM((2, LINES, 2, 128), BF16),
+            dma((8,)),
+        ],
+        compiler_params=pltpu.CompilerParams(vmem_limit_bytes=60 * 1024 * 1024),
+        name="finish",
+    )(rows, line, found)
 
 
 def solution(mesh):

time: 52.4 us -> 48.7 us (0.929)
  local copies, waits for them, and re-layouts: 4.65 us -> 0 us
  Pallas kernels: 46.9 us -> 47.9 us
    pallas_call x0 -> x1, Pallas kernels: none -> 3.63 us  [body(): pl.pallas_call(finish, out_shape=(jax.ShapeDtypeStruct((P_DEV, ORIENT, NT...]
    unnamed x1 -> x0, local copies, waits for them, and re-layouts: 2.91 us -> none
    pallas_call x1, Pallas kernels: 46.9 us -> 44.2 us  [body(): pl.pallas_call(kernel, out_shape=(jax.ShapeDtypeStruct((P_DEV, NT, ORIENT...]
    reshape x2 -> x0, local copies, waits for them, and re-layouts: 1.73 us -> none  [body(): scores = scores.reshape(P_DEV, NT, ORIENT, NT).transpose(0, 2, 1, 3)]
where the time goes in v5:
time: 48.7 us; the launch traced here: 48.5 us
  Pallas kernels  47.9 us (98%)
  between operations  0.64 us (1%)
    pallas_call x1, Pallas kernels, body(): pl.pallas_call(kernel, out_shape=(jax.ShapeDtypeStruct((P_DEV, NT, ORIENT...  44.2 us
    pallas_call x1, Pallas kernels, body(): pl.pallas_call(finish, out_shape=(jax.ShapeDtypeStruct((P_DEV, ORIENT, NT...  3.63 us

profile of v5, /device:TPU:1, one launch (start us, length us, event | category | flops | bytes accessed | tf_op | source)
XLA Modules:
  0.0 48.5 jit_solution(9315689222054347294)
XLA Ops:
  0.6 44.2 %cryo.1 = (f32[4,32,128]{2,1,0:T(8,128)}, bf16[4,2,16,256]{3,2,1,0:T(8,128)(2,1)}, s32[8,128]{1,0:T(8,128)}) custom-call(s32[4,256]{1,0:T(4,128)} %lines_hbm.1, f32[512,32]{1,0:T(8,128)} %bitcast.1, f32[4]{0:T(128)} %defocus_hbm.1, s32[32]{0:T(128)} %sy_hbm.1, s32[32]{0:T(128)} %sx_hbm.1, bf16[1024,2,256]{2,1,0:T(2,128)(2,1)} %volume_hbm.1, ...), custom_call_target="tpu_custom_call" | custom-call | tf_op jit(solution)/shard_map/cryo/pallas_call | solution.py:539
  44.9 3.6 %finish.1 = (f32[4,4,32,32]{3,2,1,0:T(8,128)}, bf16[1024,2,256]{2,1,0:T(2,128)(2,1)}) custom-call(bf16[4,2,16,256]{3,2,1,0:T(8,128)(2,1)} %get-tuple-element.5.fin_ref, s32[8,128]{1,0:T(8,128)} %get-tuple-element.6.line_ref, f32[4,32,128]{2,1,0:T(8,128)} %get-tuple-element.7.found_ref), custom_call_target="tpu_custom_call" | custom-call | tf_op jit(solution)/shard_map/finish/pallas_call | solution.py:611

commit v6 on v5

--- a/solution.py
+++ b/solution.py
@@ -175,24 +175,27 @@
             jnp.sum(jnp.where(mine, local[o : o + 1], 0.0), axis=1, keepdims=True)
         )
     own_line = jnp.concatenate(own_line, 0).astype(jnp.int32)
-    half_line = jnp.where(c == 0, own_line[0 : 2 * OWNED], own_line[2 * OWNED :])
-    column = iota((2 * OWNED, 2 * LINES), 1)
-    gather[0 : 2 * OWNED] = (column == 2 * half_line).astype(F32).astype(BF16)
-    gather[2 * OWNED :] = (column == 2 * half_line + 1).astype(F32).astype(BF16)
+    o_own = 2 * c + z % 2
+    first_line = own_line[0:OWNED]
+    for o in range(1, ORIENT):
+        first_line = jnp.where(o_own == o, own_line[o * OWNED : (o + 1) * OWNED], first_line)
+    column = iota((OWNED, 2 * LINES), 1)
+    gather[0:OWNED] = (column == 2 * first_line).astype(F32).astype(BF16)
+    gather[OWNED:] = (column == 2 * first_line + 1).astype(F32).astype(BF16)
 
     for j in range(2):
         loads[j].wait()
         picked = dot(gather[...], vbuf.at[j].reshape(2 * LINES, 128)[...]).astype(BF16)
         for part in range(2):
             at = slice(part * KS + j * 128, part * KS + j * 128 + 128)
-            own[:, at] = picked[part * 32 : part * 32 + 32]
+            own[:, at] = picked[part * OWNED : part * OWNED + OWNED]
 
     pl.semaphore_wait(barrier, SLABS - 1 + ZS - 1 + 3 + 1)
 
     def slab_copy(k):
         return pltpu.make_async_remote_copy(
             src_ref=own,
-            dst_ref=arrived.at[c, slab],
+            dst_ref=arrived.at[o_own, slab],
             send_sem=s_send.at[0],
             recv_sem=s_recv.at[0],
             device_id=slab_peer(k),
@@ -204,7 +207,7 @@
         return carry
 
     lax.fori_loop(1, SLABS, send_slab, 0)
-    arrived[c, slab] = own[...]
+    arrived[o_own, slab] = own[...]
 
     small[1].wait()
     small[2].wait()
@@ -347,6 +350,29 @@
 
     lax.fori_loop(0, 2, keep, 0)
 
+    def wait_rows(n, sem):
+        part = arrived.at[0, pl.ds(0, n)]
+        pltpu.make_async_copy(part, part, sem).wait()
+
+    def pass_rows(o, sem, first=0, n=SLABS, to=partner):
+        part = arrived.at[o, pl.ds(first, n)]
+        return pltpu.make_async_remote_copy(
+            src_ref=part,
+            dst_ref=part,
+            send_sem=s_send.at[sem],
+            recv_sem=s_recv.at[sem],
+            device_id=to,
+            device_id_type=MESH,
+        )
+
+    wait_rows(SLABS - 1, s_recv.at[0])
+    to_up = pass_rows(o_own, 2, 0, 8, z_peer(1))
+    to_down = pass_rows(o_own, 3, 8, 8, z_peer(ZS - 1))
+    to_partner = pass_rows(o_own, 1)
+    to_up.start()
+    to_down.start()
+    to_partner.start()
+
     for o in range(ORIENT):
         at_s = owner[o : o + 1] * OWNED + ranks[o]
         place_s[o] = (iota((KS, KS), 0) == at_s).astype(F32).astype(BF16)
@@ -354,20 +380,20 @@
     for o in range(ORIENT):
         cos_o = jnp.where(group == o, cos_x, 0.0).astype(BF16)
         sin_o = jnp.where(group == o, sin_x, 0.0).astype(BF16)
-        at = (o % 2) * 2 * KS
-        fx[o // 2, at : at + KS, 0:128] = cos_o
-        fx[o // 2, at : at + KS, 128:] = -sin_o
-        fx[o // 2, at + KS : at + 2 * KS, 0:128] = sin_o
-        fx[o // 2, at + KS : at + 2 * KS, 128:] = cos_o
+        at = (o // 2) * 2 * KS
+        fx[o % 2, at : at + KS, 0:128] = cos_o
+        fx[o % 2, at : at + KS, 128:] = -sin_o
+        fx[o % 2, at + KS : at + 2 * KS, 0:128] = sin_o
+        fx[o % 2, at + KS : at + 2 * KS, 128:] = cos_o
     table_y = jnp.concatenate([cos_y.T[0:NT], sin_y.T[0:NT]], 1) * (1.0 / KS)
     fy_hi = table_y.astype(BF16)
     fy[0:NT] = fy_hi
     fy[NT:] = (table_y - fy_hi.astype(F32)).astype(BF16)
 
-    def correlate(half, first):
+    def correlate(parity, first):
         for j in range(2):
-            rows_s = arrived[half, :, j * OWNED : (j + 1) * OWNED, :].reshape(KS, 2 * KS)
-            su[j] = dot_t(place_s[2 * half + j], rows_s)
+            o = 2 * j + parity
+            su[j] = dot_t(place_s[o], arrived[o].reshape(KS, 2 * KS))
         for block in range(2):
             at = slice(block * 128, block * 128 + 128)
             for p in range(P_DEV):
@@ -379,7 +405,7 @@
                     s_im = su[j, at, KS:]
                     q.append((s_re * c_re + s_im * c_im).astype(BF16))
                     q.append((s_re * c_im - s_im * c_re).astype(BF16))
-                part = dot(jnp.concatenate(q, 1), fx[half])
+                part = dot(jnp.concatenate(q, 1), fx[parity])
                 if first:
                     zacc[p, at] = part
                 else:
@@ -390,6 +416,8 @@
     line_ref[...] = line_row
     outs = [pltpu.make_async_copy(line_ref, line_hbm, out_sem.at[0])]
     outs[0].start()
+    wait_rows(SLABS, s_recv.at[1])
+    correlate(z % 2, True)
     def pass_on(j, carry):
         pltpu.make_async_copy(
             xrecv.at[j, pl.ds(0, 3)], xrecv.at[j, pl.ds(0, 3)], x_recv.at[j]
@@ -411,19 +439,10 @@
         return carry
 
     lax.fori_loop(0, 2, pass_on, 0)
-    pltpu.make_async_copy(
-        arrived.at[0, pl.ds(0, SLABS - 1)], arrived.at[0, pl.ds(0, SLABS - 1)], s_recv.at[0]
-    ).wait()
-    forward = pltpu.make_async_remote_copy(
-        src_ref=arrived.at[c],
-        dst_ref=arrived.at[c],
-        send_sem=s_send.at[1],
-        recv_sem=s_recv.at[1],
-        device_id=partner,
-        device_id_type=MESH,
-    )
-    forward.start()
-    correlate(c, True)
+    wait_rows(8, s_recv.at[2])
+    wait_rows(8, s_recv.at[3])
+    to_partner_too = pass_rows(2 * c + 1 - z % 2, 4)
+    to_partner_too.start()
 
     def spread(j, carry):
         pltpu.make_async_copy(
@@ -443,8 +462,8 @@
         return carry
 
     lax.fori_loop(0, 2, spread, 0)
-    forward.wait_recv()
-    correlate(1 - c, False)
+    wait_rows(SLABS, s_recv.at[4])
+    correlate(1 - z % 2, False)
 
     place = x_lo * 2 + c
     for j in range(2):
@@ -481,10 +500,9 @@
     outs.append(pltpu.make_async_copy(fin, rows_hbm, out_sem.at[2]))
     outs[2].start()
 
-    pltpu.make_async_copy(
-        arrived.at[0, pl.ds(0, SLABS - 1)], arrived.at[0, pl.ds(0, SLABS - 1)], s_send.at[0]
-    ).wait()
-    forward.wait_send()
+    wait_rows(SLABS - 1, s_send.at[0])
+    for sent_rows in (to_partner, to_up, to_down, to_partner_too):
+        sent_rows.wait_send()
     for j in range(2):
         pair_copy(j).wait_send()
     for j in range(2):
@@ -503,7 +521,21 @@
         out.wait()
 
 
-def finish(fin_ref, line_ref, found_ref, scores_ref, update_hbm, rows, buf, out_sem):
+def finish(
+    fin_hbm, line_hbm, found_hbm, scores_hbm, update_hbm,
+    fin_ref, line_ref, found_ref, scores_ref, insert, rows, buf, in_sem, out_sem,
+):
+    loads = [
+        pltpu.make_async_copy(src, dst, in_sem.at[i])
+        for i, (src, dst) in enumerate(
+            ((line_hbm, line_ref), (fin_hbm, fin_ref), (found_hbm, found_ref))
+        )
+    ]
+    for load in loads:
+        load.start()
+    loads[0].wait()
+    insert[...] = (iota((2 * LINES, 128), 0) == line_ref[0:1]).astype(F32).astype(BF16)
+    loads[1].wait()
     for o in range(ORIENT):
         for r in range(2):
             got = fin_ref[r * 2 + o // 2, o % 2].astype(F32)
@@ -514,8 +546,8 @@
     outs = []
     for piece in range(4):
         of = pl.ds(piece * 256, 256)
-        insert = iota((512, 128), 0) + piece * 512 == line_ref[0:1]
-        placed = dot(insert.astype(F32).astype(BF16), rows_bf16).astype(BF16)
+        at = slice(piece * 512, piece * 512 + 512)
+        placed = dot(insert[at], rows_bf16).astype(BF16)
         for j in range(2):
             buf.at[j, of].reshape(512, 128)[...] = placed[:, j * 128 : j * 128 + 128]
             outs.append(
@@ -526,14 +558,16 @@
                 )
             )
             outs[-1].start()
+    loads[2].wait()
     for o in range(ORIENT):
         scores_ref[:, o] = found_ref[:, :, o * NT : (o + 1) * NT]
+    outs.append(pltpu.make_async_copy(scores_ref, scores_hbm, out_sem.at[8]))
+    outs[-1].start()
     for out in outs:
         out.wait()
 
 
 def body(volume, images, defocus, soft_weights, slice_lines, shift_y, shift_x):
-    vmem = pl.BlockSpec(memory_space=pltpu.VMEM)
     hbm = pl.BlockSpec(memory_space=pltpu.HBM)
     dma = pltpu.SemaphoreType.DMA
     found, rows, line = pl.pallas_call(
@@ -556,9 +590,9 @@
             pltpu.VMEM((2, LINES, 2, 128), BF16),
             pltpu.VMEM((2, P_DEV, KS, 2, 128), BF16),
             pltpu.VMEM((2 * KS, 128), F32),
-            pltpu.VMEM((2 * OWNED, 2 * KS), BF16),
-            pltpu.VMEM((2, SLABS, 2 * OWNED, 2 * KS), BF16),
-            pltpu.VMEM((4 * OWNED, 2 * LINES), BF16),
+            pltpu.VMEM((OWNED, 2 * KS), BF16),
+            pltpu.VMEM((ORIENT, SLABS, OWNED, 2 * KS), BF16),
+            pltpu.VMEM((2 * OWNED, 2 * LINES), BF16),
             pltpu.VMEM((ORIENT, KS, KS), BF16),
             pltpu.VMEM((ORIENT, KS, KS), BF16),
             pltpu.VMEM((2, 4 * KS, 256), BF16),
@@ -582,8 +616,8 @@
             dma((5,)),
             dma((4,)),
             dma((3,)),
-            dma((2,)),
-            dma((2,)),
+            dma((5,)),
+            dma((5,)),
             dma((2,)),
             dma((2,)),
             dma((2,)),
@@ -614,12 +648,18 @@
             jax.ShapeDtypeStruct((P_DEV, ORIENT, NT, NT), F32),
             jax.ShapeDtypeStruct((LINES, 2, KS), BF16),
         ),
-        in_specs=[vmem] * 3,
-        out_specs=(vmem, hbm),
+        in_specs=[hbm] * 3,
+        out_specs=(hbm, hbm),
         scratch_shapes=[
+            pltpu.VMEM((4, 2, 16, KS), BF16),
+            pltpu.VMEM((8, 128), jnp.int32),
+            pltpu.VMEM((P_DEV, NT, ORIENT * NT), F32),
+            pltpu.VMEM((P_DEV, ORIENT, NT, NT), F32),
+            pltpu.VMEM((2 * LINES, 2 * ORIENT * OWNED), BF16),
             pltpu.VMEM((2 * ORIENT * OWNED, KS), F32),
             pltpu.VMEM((2, LINES, 2, 128), BF16),
-            dma((8,)),
+            dma((3,)),
+            dma((9,)),
         ],
         compiler_params=pltpu.CompilerParams(vmem_limit_bytes=60 * 1024 * 1024),
         name="finish",

time: 48.7 us -> 46.2 us (0.949)
  Pallas kernels: 47.9 us -> 45.4 us
    pallas_call x1, Pallas kernels: 44.2 us -> 42.4 us  [body(): pl.pallas_call(kernel, out_shape=(jax.ShapeDtypeStruct((P_DEV, NT, ORIENT...]
    pallas_call x1, Pallas kernels: 3.63 us -> 3.05 us  [body(): pl.pallas_call(finish, out_shape=(jax.ShapeDtypeStruct((P_DEV, ORIENT, NT...]
where the time goes in v6:
time: 46.2 us; the launch traced here: 46 us
  Pallas kernels  45.4 us (98%)
  between operations  0.64 us (1%)
    pallas_call x1, Pallas kernels, body(): pl.pallas_call(kernel, out_shape=(jax.ShapeDtypeStruct((P_DEV, NT, ORIENT...  42.4 us
    pallas_call x1, Pallas kernels, body(): pl.pallas_call(finish, out_shape=(jax.ShapeDtypeStruct((P_DEV, ORIENT, NT...  3.05 us

profile of v6, /device:TPU:1, one launch (start us, length us, event | category | flops | bytes accessed | tf_op | source)
XLA Modules:
  0.0 46.0 jit_solution(13865923959353843260)
XLA Ops:
  0.6 42.4 %cryo.1 = (f32[4,32,128]{2,1,0:T(8,128)}, bf16[4,2,16,256]{3,2,1,0:T(8,128)(2,1)}, s32[8,128]{1,0:T(8,128)}) custom-call(s32[4,256]{1,0:T(4,128)} %lines_hbm.1, f32[512,32]{1,0:T(8,128)} %bitcast.1, f32[4]{0:T(128)} %defocus_hbm.1, s32[32]{0:T(128)} %sy_hbm.1, s32[32]{0:T(128)} %sx_hbm.1, bf16[1024,2,256]{2,1,0:T(2,128)(2,1)} %volume_hbm.1, ...), custom_call_target="tpu_custom_call" | custom-call | tf_op jit(solution)/shard_map/cryo/pallas_call | solution.py:573
  43.0 3.0 %finish.1 = (f32[4,4,32,32]{3,2,1,0:T(8,128)}, bf16[1024,2,256]{2,1,0:T(2,128)(2,1)}) custom-call(bf16[4,2,16,256]{3,2,1,0:T(8,128)(2,1)} %get-tuple-element.5.fin_hbm, s32[8,128]{1,0:T(8,128)} %get-tuple-element.6.line_hbm, f32[4,32,128]{2,1,0:T(8,128)} %get-tuple-element.7.found_hbm), custom_call_target="tpu_custom_call" | custom-call | tf_op jit(solution)/shard_map/finish/pallas_call | solution.py:645

commit v7 on v6

--- a/solution.py
+++ b/solution.py
@@ -148,8 +148,8 @@
         greet(z_peer(k))
         return carry
 
-    lax.fori_loop(1, SLABS, greet_slab, 0)
-    lax.fori_loop(1, ZS, greet_z, 0)
+    lax.fori_loop(1, SLABS, greet_slab, 0, unroll=True)
+    lax.fori_loop(1, ZS, greet_z, 0, unroll=True)
     for k in range(1, 4):
         greet(group_peer(k))
     greet((dom, y * 2 + 1 - x_hi))
@@ -206,7 +206,7 @@
         slab_copy(k).start()
         return carry
 
-    lax.fori_loop(1, SLABS, send_slab, 0)
+    lax.fori_loop(1, SLABS, send_slab, 0, unroll=True)
     arrived[o_own, slab] = own[...]
 
     small[1].wait()
@@ -344,7 +344,7 @@
             x_copy(j, k).start()
             return inner
 
-        lax.fori_loop(1, 4, send_x, 0)
+        lax.fori_loop(1, 4, send_x, 0, unroll=True)
         xrecv[j, x] = xsend[j, x]
         return carry
 
@@ -434,7 +434,7 @@
             y_copy(j, k).start()
             return inner
 
-        lax.fori_loop(1, YS, send_y, 0)
+        lax.fori_loop(1, YS, send_y, 0, unroll=True)
         yrecv[j, y] = ysend[j, y]
         return carry
 
@@ -457,7 +457,7 @@
             z_copy(j, k).start()
             return inner
 
-        lax.fori_loop(1, ZS, send_z, 0)
+        lax.fori_loop(1, ZS, send_z, 0, unroll=True)
         zrecv[j, z] = zsend[j]
         return carry
 

time: 46.2 us -> 46.3 us (level)
  no operation moved by 1% of the time
where the time goes in v7:
time: 46.3 us; the launch traced here: 46.1 us
  Pallas kernels  45.4 us (98%)
  between operations  0.64 us (1%)
    pallas_call x1, Pallas kernels, body(): pl.pallas_call(kernel, out_shape=(jax.ShapeDtypeStruct((P_DEV, NT, ORIENT...  42.4 us
    pallas_call x1, Pallas kernels, body(): pl.pallas_call(finish, out_shape=(jax.ShapeDtypeStruct((P_DEV, ORIENT, NT...  3.05 us

profile of v7, /device:TPU:1, one launch (start us, length us, event | category | flops | bytes accessed | tf_op | source)
XLA Modules:
  0.0 46.1 jit_solution(688750797507666035)
XLA Ops:
  0.6 42.4 %cryo.1 = (f32[4,32,128]{2,1,0:T(8,128)}, bf16[4,2,16,256]{3,2,1,0:T(8,128)(2,1)}, s32[8,128]{1,0:T(8,128)}) custom-call(s32[4,256]{1,0:T(4,128)} %lines_hbm.1, f32[512,32]{1,0:T(8,128)} %bitcast.1, f32[4]{0:T(128)} %defocus_hbm.1, s32[32]{0:T(128)} %sy_hbm.1, s32[32]{0:T(128)} %sx_hbm.1, bf16[1024,2,256]{2,1,0:T(2,128)(2,1)} %volume_hbm.1, ...), custom_call_target="tpu_custom_call" | custom-call | tf_op jit(solution)/shard_map/cryo/pallas_call | solution.py:573
  43.0 3.0 %finish.1 = (f32[4,4,32,32]{3,2,1,0:T(8,128)}, bf16[1024,2,256]{2,1,0:T(2,128)(2,1)}) custom-call(bf16[4,2,16,256]{3,2,1,0:T(8,128)(2,1)} %get-tuple-element.5.fin_hbm, s32[8,128]{1,0:T(8,128)} %get-tuple-element.6.line_hbm, f32[4,32,128]{2,1,0:T(8,128)} %get-tuple-element.7.found_hbm), custom_call_target="tpu_custom_call" | custom-call | tf_op jit(solution)/shard_map/finish/pallas_call | solution.py:645

commit v8 on v6

--- a/solution.py
+++ b/solution.py
@@ -189,25 +189,6 @@
         for part in range(2):
             at = slice(part * KS + j * 128, part * KS + j * 128 + 128)
             own[:, at] = picked[part * OWNED : part * OWNED + OWNED]
-
-    pl.semaphore_wait(barrier, SLABS - 1 + ZS - 1 + 3 + 1)
-
-    def slab_copy(k):
-        return pltpu.make_async_remote_copy(
-            src_ref=own,
-            dst_ref=arrived.at[o_own, slab],
-            send_sem=s_send.at[0],
-            recv_sem=s_recv.at[0],
-            device_id=slab_peer(k),
-            device_id_type=MESH,
-        )
-
-    def send_slab(k, carry):
-        slab_copy(k).start()
-        return carry
-
-    lax.fori_loop(1, SLABS, send_slab, 0)
-    arrived[o_own, slab] = own[...]
 
     small[1].wait()
     small[2].wait()
@@ -329,10 +310,32 @@
 
     def give(j, carry):
         sent[j] = placed_term(2 * (1 - c) + j).astype(BF16)
-        pair_copy(j).start()
         return carry
 
     lax.fori_loop(0, 2, give, 0)
+
+    pl.semaphore_wait(barrier, SLABS - 1 + ZS - 1 + 3 + 1)
+
+    pair_copy(0).start()
+    pair_copy(1).start()
+
+    def slab_copy(k):
+        return pltpu.make_async_remote_copy(
+            src_ref=own,
+            dst_ref=arrived.at[o_own, slab],
+            send_sem=s_send.at[0],
+            recv_sem=s_recv.at[0],
+            device_id=slab_peer(k),
+            device_id_type=MESH,
+        )
+
+    def send_slab(k, carry):
+        slab_copy(k).start()
+        return carry
+
+    lax.fori_loop(1, SLABS, send_slab, 0)
+    arrived[o_own, slab] = own[...]
+
 
     def keep(j, carry):
         mine = placed_term(2 * c + j)

time: 46.2 us -> 46.2 us (level)
  no operation moved by 1% of the time
where the time goes in v8:
time: 46.2 us; the launch traced here: 46 us
  Pallas kernels  45.3 us (98%)
  between operations  0.64 us (1%)
    pallas_call x1, Pallas kernels, body(): pl.pallas_call(kernel, out_shape=(jax.ShapeDtypeStruct((P_DEV, NT, ORIENT...  42.3 us
    pallas_call x1, Pallas kernels, body(): pl.pallas_call(finish, out_shape=(jax.ShapeDtypeStruct((P_DEV, ORIENT, NT...  3.05 us

profile of v8, /device:TPU:1, one launch (start us, length us, event | category | flops | bytes accessed | tf_op | source)
XLA Modules:
  0.0 46.0 jit_solution(6402298128954668133)
XLA Ops:
  0.6 42.3 %cryo.1 = (f32[4,32,128]{2,1,0:T(8,128)}, bf16[4,2,16,256]{3,2,1,0:T(8,128)(2,1)}, s32[8,128]{1,0:T(8,128)}) custom-call(s32[4,256]{1,0:T(4,128)} %lines_hbm.1, f32[512,32]{1,0:T(8,128)} %bitcast.1, f32[4]{0:T(128)} %defocus_hbm.1, s32[32]{0:T(128)} %sy_hbm.1, s32[32]{0:T(128)} %sx_hbm.1, bf16[1024,2,256]{2,1,0:T(2,128)(2,1)} %volume_hbm.1, ...), custom_call_target="tpu_custom_call" | custom-call | tf_op jit(solution)/shard_map/cryo/pallas_call | solution.py:576
  42.9 3.0 %finish.1 = (f32[4,4,32,32]{3,2,1,0:T(8,128)}, bf16[1024,2,256]{2,1,0:T(2,128)(2,1)}) custom-call(bf16[4,2,16,256]{3,2,1,0:T(8,128)(2,1)} %get-tuple-element.5.fin_hbm, s32[8,128]{1,0:T(8,128)} %get-tuple-element.6.line_hbm, f32[4,32,128]{2,1,0:T(8,128)} %get-tuple-element.7.found_hbm), custom_call_target="tpu_custom_call" | custom-call | tf_op jit(solution)/shard_map/finish/pallas_call | solution.py:648

commit v9 on v8

--- a/solution.py
+++ b/solution.py
@@ -368,14 +368,6 @@
             device_id_type=MESH,
         )
 
-    wait_rows(SLABS - 1, s_recv.at[0])
-    to_up = pass_rows(o_own, 2, 0, 8, z_peer(1))
-    to_down = pass_rows(o_own, 3, 8, 8, z_peer(ZS - 1))
-    to_partner = pass_rows(o_own, 1)
-    to_up.start()
-    to_down.start()
-    to_partner.start()
-
     for o in range(ORIENT):
         at_s = owner[o : o + 1] * OWNED + ranks[o]
         place_s[o] = (iota((KS, KS), 0) == at_s).astype(F32).astype(BF16)
@@ -419,8 +411,14 @@
     line_ref[...] = line_row
     outs = [pltpu.make_async_copy(line_ref, line_hbm, out_sem.at[0])]
     outs[0].start()
-    wait_rows(SLABS, s_recv.at[1])
-    correlate(z % 2, True)
+    wait_rows(SLABS - 1, s_recv.at[0])
+    to_up = pass_rows(o_own, 2, 0, 8, z_peer(1))
+    to_down = pass_rows(o_own, 3, 8, 8, z_peer(ZS - 1))
+    to_partner = pass_rows(o_own, 1)
+    to_up.start()
+    to_down.start()
+    to_partner.start()
+
     def pass_on(j, carry):
         pltpu.make_async_copy(
             xrecv.at[j, pl.ds(0, 3)], xrecv.at[j, pl.ds(0, 3)], x_recv.at[j]
@@ -442,6 +440,8 @@
         return carry
 
     lax.fori_loop(0, 2, pass_on, 0)
+    wait_rows(SLABS, s_recv.at[1])
+    correlate(z % 2, True)
     wait_rows(8, s_recv.at[2])
     wait_rows(8, s_recv.at[3])
     to_partner_too = pass_rows(2 * c + 1 - z % 2, 4)

time: 46.2 us -> 46.3 us (level)
  no operation moved by 1% of the time
where the time goes in v9:
time: 46.3 us; the launch traced here: 46.1 us
  Pallas kernels  45.5 us (98%)
  between operations  0.64 us (1%)
    pallas_call x1, Pallas kernels, body(): pl.pallas_call(kernel, out_shape=(jax.ShapeDtypeStruct((P_DEV, NT, ORIENT...  42.4 us
    pallas_call x1, Pallas kernels, body(): pl.pallas_call(finish, out_shape=(jax.ShapeDtypeStruct((P_DEV, ORIENT, NT...  3.05 us

profile of v9, /device:TPU:1, one launch (start us, length us, event | category | flops | bytes accessed | tf_op | source)
XLA Modules:
  0.0 46.1 jit_solution(13746451466251228335)
XLA Ops:
  0.6 42.4 %cryo.1 = (f32[4,32,128]{2,1,0:T(8,128)}, bf16[4,2,16,256]{3,2,1,0:T(8,128)(2,1)}, s32[8,128]{1,0:T(8,128)}) custom-call(s32[4,256]{1,0:T(4,128)} %lines_hbm.1, f32[512,32]{1,0:T(8,128)} %bitcast.1, f32[4]{0:T(128)} %defocus_hbm.1, s32[32]{0:T(128)} %sy_hbm.1, s32[32]{0:T(128)} %sx_hbm.1, bf16[1024,2,256]{2,1,0:T(2,128)(2,1)} %volume_hbm.1, ...), custom_call_target="tpu_custom_call" | custom-call | tf_op jit(solution)/shard_map/cryo/pallas_call | solution.py:576
  43.1 3.0 %finish.1 = (f32[4,4,32,32]{3,2,1,0:T(8,128)}, bf16[1024,2,256]{2,1,0:T(2,128)(2,1)}) custom-call(bf16[4,2,16,256]{3,2,1,0:T(8,128)(2,1)} %get-tuple-element.5.fin_hbm, s32[8,128]{1,0:T(8,128)} %get-tuple-element.6.line_hbm, f32[4,32,128]{2,1,0:T(8,128)} %get-tuple-element.7.found_hbm), custom_call_target="tpu_custom_call" | custom-call | tf_op jit(solution)/shard_map/finish/pallas_call | solution.py:648

commit v10 on v9

--- a/solution.py
+++ b/solution.py
@@ -29,10 +29,6 @@
     return jnp.dot(a, b, preferred_element_type=F32)
 
 
-def dot_t(a, b):
-    return lax.dot_general(a, b, (((0,), (0,)), ((), ())), preferred_element_type=F32)
-
-
 def poly_sin_cos(r):
     s = r * r
     sin = r * (1.0 + s * (-1 / 6 + s * (1 / 120 + s * (-1 / 5040 + s * (1 / 362880)))))
@@ -74,7 +70,8 @@
     scores_hbm, rows_hbm, line_hbm,
     scores_ref, line_ref, lines_ref, weights_ref, defocus_ref, sy_ref, sx_ref,
     vbuf, ibuf, split, own, arrived, gather, place_s, place_t,
-    fx, ephase, fy, hs, cx, term, sent, landed, xsend, xrecv, ysend, yrecv, zsend, zrecv,
+    fx, ephase, fy, hs, cx, term, sent, landed, xsend, xrecv, x1send, x1recv, ysend, yrecv,
+    y1send, y1recv, zsend, zrecv,
     fin, tile_y, zacc, su,
     small_sem, in_sem, out_sem, s_send, s_recv, p_send, p_recv, x_send, x_recv, z_send, z_recv,
     y_send, y_recv, f_send, f_recv,
@@ -202,8 +199,11 @@
     sin_x, cos_x = turns_sin_cos(freq * row_x[0:1])
     sin_y, cos_y = turns_sin_cos(freq * row_y[0:1])
     wide_lane = iota((KS, 128), 1)
-    ephase[0:KS] = jnp.where(wide_lane < NT, cos_y, -sin_y)[:, : 2 * NT].astype(BF16)
-    ephase[KS:] = jnp.where(wide_lane < NT, sin_y, cos_y)[:, : 2 * NT].astype(BF16)
+    e_re = jnp.where(wide_lane < NT, cos_y, -sin_y)[:, : 2 * NT].astype(BF16)
+    e_im = jnp.where(wide_lane < NT, sin_y, cos_y)[:, : 2 * NT].astype(BF16)
+    for block in range(2):
+        ephase[block, 0:128] = e_re[block * 128 : block * 128 + 128]
+        ephase[block, 128:] = e_im[block * 128 : block * 128 + 128]
     t_cos = cos_x.T[0:NT]
     t_sin = sin_x.T[0:NT]
     table = jnp.concatenate([t_cos, t_sin], 1)
@@ -220,7 +220,10 @@
     for o in range(ORIENT):
         rank = ranks[o]
         row = owner[o : o + 1]
-        at_t = (row & 1) * 128 + (rank >> 3) * 64 + (row >> 1) * 8 + (rank & 7)
+        if o % 2 == 0:
+            at_t = (row & 1) * 128 + (rank >> 3) * 64 + (row >> 1) * 8 + (rank & 7)
+        else:
+            at_t = (row >> 1) * 32 + (row & 1) * 16 + (rank >> 3) * 8 + (rank & 7)
         place_t[o] = (iota((KS, KS), 0) == at_t).astype(F32).astype(BF16)
 
     freq_row = (iota((8, KS), 1) - HALF).astype(F32)
@@ -237,12 +240,14 @@
     loads[2].wait()
     loads[3].wait()
     for p in range(P_DEV):
+        sin_p = jnp.broadcast_to(sin_col[:, p : p + 1], (KS, 128))
+        cos_p = jnp.broadcast_to(cos_col[:, p : p + 1], (KS, 128))
         for j in range(2):
             at = slice(j * 128, j * 128 + 128)
             split[...] = ibuf.at[j, p].reshape(2 * KS, 128)[...].astype(F32)
             ctf = (
-                sin_col[:, p : p + 1] * u_row[p : p + 1, at]
-                + cos_col[:, p : p + 1] * v_row[p : p + 1, at]
+                sin_p * u_row[p : p + 1, at]
+                + cos_p * v_row[p : p + 1, at]
             )
             cx[p, 0, :, at] = ctf * split[pl.ds(0, KS, stride=2), :]
             cx[p, 1, :, at] = ctf * split[pl.ds(1, KS, stride=2), :]
@@ -250,12 +255,12 @@
     def placed_term(o):
         for block in range(2):
             at = slice(block * 128, block * 128 + 128)
-            low = slice(KS + block * 128, KS + block * 128 + 128)
             t_re = None
             for p in range(P_DEV):
                 table_h = hs[p * ORIENT + o]
-                g_re = dot(ephase[at], table_h)
-                g_im = dot(ephase[low], table_h)
+                g = dot(ephase[block], table_h)
+                g_re = g[0:128]
+                g_im = g[128:]
                 c_re = cx[p, 0, at]
                 c_im = cx[p, 1, at]
                 if t_re is None:
@@ -278,25 +283,52 @@
             device_id_type=MESH,
         )
 
-    def x_copy(j, k):
+    def x_copy(j, send, recv, k):
         return pltpu.make_async_remote_copy(
-            src_ref=xsend.at[j, lax.rem(x + k, 4)],
-            dst_ref=xrecv.at[j, x],
+            src_ref=send.at[lax.rem(x + k, 4)],
+            dst_ref=recv.at[x],
             send_sem=x_send.at[j],
             recv_sem=x_recv.at[j],
             device_id=x_peer(k),
             device_id_type=MESH,
         )
 
-    def y_copy(j, k):
+    def y_copy(j, send, recv, k):
         return pltpu.make_async_remote_copy(
-            src_ref=ysend.at[j, lax.rem(y + k, YS)],
-            dst_ref=yrecv.at[j, y],
+            src_ref=send.at[lax.rem(y + k, YS)],
+            dst_ref=recv.at[y],
             send_sem=y_send.at[j],
             recv_sem=y_recv.at[j],
             device_id=y_peer(k),
             device_id_type=MESH,
         )
+
+    def send_x(j, send, recv):
+        def start(k, carry):
+            x_copy(j, send, recv, k).start()
+            return carry
+
+        lax.fori_loop(1, 4, start, 0)
+        recv[x] = send[x]
+
+    def send_y(j, send, recv):
+        def start(k, carry):
+            y_copy(j, send, recv, k).start()
+            return carry
+
+        lax.fori_loop(1, YS, start, 0)
+        recv[y] = send[y]
+
+    def sum_of(ref, n, sem, *at):
+        part = ref.at[pl.ds(0, n - 1)]
+        pltpu.make_async_copy(part, part, sem).wait()
+        return sum_over(ref, n, *at)
+
+    def sum_over(ref, n, *at):
+        total = ref[(0,) + at].astype(F32)
+        for other in range(1, n):
+            total += ref[(other,) + at].astype(F32)
+        return total
 
     def z_copy(j, k):
         return pltpu.make_async_remote_copy(
@@ -337,21 +369,16 @@
     arrived[o_own, slab] = own[...]
 
 
-    def keep(j, carry):
+    for j in range(2):
         mine = placed_term(2 * c + j)
         pair_copy(j).wait_recv()
         both = (mine + landed[j].astype(F32)).astype(BF16)
-        xsend[j] = both.reshape(4, 64, 2 * KS)
-
-        def send_x(k, inner):
-            x_copy(j, k).start()
-            return inner
-
-        lax.fori_loop(1, 4, send_x, 0)
-        xrecv[j, x] = xsend[j, x]
-        return carry
-
-    lax.fori_loop(0, 2, keep, 0)
+        if j == 0:
+            xsend[...] = both.reshape(4, 64, 2 * KS)
+            send_x(0, xsend, xrecv)
+        else:
+            y1send[...] = both.reshape(YS, NT, 2 * KS)
+            send_y(1, y1send, y1recv)
 
     def wait_rows(n, sem):
         part = arrived.at[0, pl.ds(0, n)]
@@ -368,9 +395,10 @@
             device_id_type=MESH,
         )
 
+    at_s = [owner[o : o + 1] * OWNED + ranks[o] for o in range(ORIENT)]
+    at_s = jnp.concatenate(at_s + at_s, 0).astype(F32).T.astype(jnp.int32)
     for o in range(ORIENT):
-        at_s = owner[o : o + 1] * OWNED + ranks[o]
-        place_s[o] = (iota((KS, KS), 0) == at_s).astype(F32).astype(BF16)
+        place_s[o] = (iota((KS, KS), 1) == at_s[:, o : o + 1]).astype(F32).astype(BF16)
     group = wide_lane // NT
     for o in range(ORIENT):
         cos_o = jnp.where(group == o, cos_x, 0.0).astype(BF16)
@@ -388,7 +416,7 @@
     def correlate(parity, first):
         for j in range(2):
             o = 2 * j + parity
-            su[j] = dot_t(place_s[o], arrived[o].reshape(KS, 2 * KS))
+            su[j] = dot(place_s[o], arrived[o].reshape(KS, 2 * KS))
         for block in range(2):
             at = slice(block * 128, block * 128 + 128)
             for p in range(P_DEV):
@@ -419,27 +447,21 @@
     to_down.start()
     to_partner.start()
 
-    def pass_on(j, carry):
-        pltpu.make_async_copy(
-            xrecv.at[j, pl.ds(0, 3)], xrecv.at[j, pl.ds(0, 3)], x_recv.at[j]
-        ).wait()
-        for part in range(2):
-            at = slice(part * KS, part * KS + KS)
-            total = xrecv[j, 0, :, at].astype(F32)
-            for other in range(1, 4):
-                total += xrecv[j, other, :, at].astype(F32)
-            tile_y[:, part * 8 : part * 8 + 8] = total.reshape(YS, 8, KS)
-        ysend[j] = tile_y[...].astype(BF16)
-
-        def send_y(k, inner):
-            y_copy(j, k).start()
-            return inner
-
-        lax.fori_loop(1, YS, send_y, 0)
-        yrecv[j, y] = ysend[j, y]
-        return carry
-
-    lax.fori_loop(0, 2, pass_on, 0)
+    everything = slice(None)
+    part = xrecv.at[pl.ds(0, 3)]
+    pltpu.make_async_copy(part, part, x_recv.at[0]).wait()
+    for part in range(2):
+        total = sum_over(xrecv, 4, everything, slice(part * KS, part * KS + KS))
+        tile_y[:, part * 8 : part * 8 + 8] = total.reshape(YS, 8, KS)
+    ysend[...] = tile_y[...].astype(BF16)
+    send_y(0, ysend, yrecv)
+    part = y1recv.at[pl.ds(0, YS - 1)]
+    pltpu.make_async_copy(part, part, y_recv.at[1]).wait()
+    for part in range(2):
+        total = sum_over(y1recv, YS, everything, slice(part * KS, part * KS + KS))
+        tile_y[0:4, part * 8 : part * 8 + 8] = total.reshape(4, 8, KS)
+    x1send[...] = tile_y[0:4].astype(BF16)
+    send_x(1, x1send, x1recv)
     wait_rows(SLABS, s_recv.at[1])
     correlate(z % 2, True)
     wait_rows(8, s_recv.at[2])
@@ -447,24 +469,19 @@
     to_partner_too = pass_rows(2 * c + 1 - z % 2, 4)
     to_partner_too.start()
 
-    def spread(j, carry):
-        pltpu.make_async_copy(
-            yrecv.at[j, pl.ds(0, YS - 1)], yrecv.at[j, pl.ds(0, YS - 1)], y_recv.at[j]
-        ).wait()
-        total = yrecv[j, 0].astype(F32)
-        for other in range(1, YS):
-            total += yrecv[j, other].astype(F32)
+    for j in range(2):
+        if j == 0:
+            total = sum_of(yrecv, YS, y_recv.at[0])
+        else:
+            total = sum_of(x1recv, 4, x_recv.at[1])
         zsend[j] = total.astype(BF16)
 
-        def send_z(k, inner):
+        def send_z(k, carry):
             z_copy(j, k).start()
-            return inner
+            return carry
 
         lax.fori_loop(1, ZS, send_z, 0)
         zrecv[j, z] = zsend[j]
-        return carry
-
-    lax.fori_loop(0, 2, spread, 0)
     wait_rows(SLABS, s_recv.at[4])
     correlate(1 - z % 2, False)
 
@@ -508,17 +525,16 @@
         sent_rows.wait_send()
     for j in range(2):
         pair_copy(j).wait_send()
-    for j in range(2):
-        pltpu.make_async_copy(
-            xrecv.at[j, pl.ds(0, 3)], xrecv.at[j, pl.ds(0, 3)], x_send.at[j]
-        ).wait()
-    for j in range(2):
-        pltpu.make_async_copy(
-            yrecv.at[j, pl.ds(0, YS - 1)], yrecv.at[j, pl.ds(0, YS - 1)], y_send.at[j]
-        ).wait()
-        pltpu.make_async_copy(
-            zrecv.at[j, pl.ds(0, ZS - 1)], zrecv.at[j, pl.ds(0, ZS - 1)], z_send.at[j]
-        ).wait()
+    for ref, n, sem in (
+        (xrecv, 4, x_send.at[0]),
+        (x1recv, 4, x_send.at[1]),
+        (yrecv, YS, y_send.at[0]),
+        (y1recv, YS, y_send.at[1]),
+        (zrecv.at[0], ZS, z_send.at[0]),
+        (zrecv.at[1], ZS, z_send.at[1]),
+    ):
+        part = ref.at[pl.ds(0, n - 1)]
+        pltpu.make_async_copy(part, part, sem).wait()
     pltpu.make_async_copy(fin.at[pl.ds(0, 3)], fin.at[pl.ds(0, 3)], f_send.at[0]).wait()
     for out in outs:
         out.wait()
@@ -599,17 +615,21 @@
             pltpu.VMEM((ORIENT, KS, KS), BF16),
             pltpu.VMEM((ORIENT, KS, KS), BF16),
             pltpu.VMEM((2, 4 * KS, 256), BF16),
-            pltpu.VMEM((2 * KS, 2 * NT), BF16),
+            pltpu.VMEM((2, KS, 2 * NT), BF16),
             pltpu.VMEM((2 * NT, 2 * KS), BF16),
             pltpu.VMEM((P_DEV * ORIENT, 2 * NT, KS), BF16),
             pltpu.VMEM((P_DEV, 2, KS, KS), F32),
             pltpu.VMEM((KS, 2 * KS), BF16),
             pltpu.VMEM((2, KS, 2 * KS), BF16),
             pltpu.VMEM((2, KS, 2 * KS), BF16),
-            pltpu.VMEM((2, 4, 64, 2 * KS), BF16),
-            pltpu.VMEM((2, 4, 64, 2 * KS), BF16),
-            pltpu.VMEM((2, YS, 16, KS), BF16),
-            pltpu.VMEM((2, YS, 16, KS), BF16),
+            pltpu.VMEM((4, 64, 2 * KS), BF16),
+            pltpu.VMEM((4, 64, 2 * KS), BF16),
+            pltpu.VMEM((4, 16, KS), BF16),
+            pltpu.VMEM((4, 16, KS), BF16),
+            pltpu.VMEM((YS, 16, KS), BF16),
+            pltpu.VMEM((YS, 16, KS), BF16),
+            pltpu.VMEM((YS, NT, 2 * KS), BF16),
+            pltpu.VMEM((YS, NT, 2 * KS), BF16),
             pltpu.VMEM((2, 16, KS), BF16),
             pltpu.VMEM((2, ZS, 16, KS), BF16),
             pltpu.VMEM((4, 2, 16, KS), BF16),

time: 46.3 us -> 48.9 us (1.056)
  Pallas kernels: 45.5 us -> 48 us
    pallas_call x1, Pallas kernels: 42.4 us -> 45 us  [body(): pl.pallas_call(kernel, out_shape=(jax.ShapeDtypeStruct((P_DEV, NT, ORIENT...]
where the time goes in v10:
time: 48.9 us; the launch traced here: 48.7 us
  Pallas kernels  48 us (98%)
  between operations  0.64 us (1%)
    pallas_call x1, Pallas kernels, body(): pl.pallas_call(kernel, out_shape=(jax.ShapeDtypeStruct((P_DEV, NT, ORIENT...  45 us
    pallas_call x1, Pallas kernels, body(): pl.pallas_call(finish, out_shape=(jax.ShapeDtypeStruct((P_DEV, ORIENT, NT...  3.05 us

profile of v10, /device:TPU:1, one launch (start us, length us, event | category | flops | bytes accessed | tf_op | source)
XLA Modules:
  0.0 48.7 jit_solution(8574000725307251769)
XLA Ops:
  0.6 45.0 %cryo.1 = (f32[4,32,128]{2,1,0:T(8,128)}, bf16[4,2,16,256]{3,2,1,0:T(8,128)(2,1)}, s32[8,128]{1,0:T(8,128)}) custom-call(s32[4,256]{1,0:T(4,128)} %lines_hbm.1, f32[512,32]{1,0:T(8,128)} %bitcast.1, f32[4]{0:T(128)} %defocus_hbm.1, s32[32]{0:T(128)} %sy_hbm.1, s32[32]{0:T(128)} %sx_hbm.1, bf16[1024,2,256]{2,1,0:T(2,128)(2,1)} %volume_hbm.1, ...), custom_call_target="tpu_custom_call" | custom-call | tf_op jit(solution)/shard_map/cryo/pallas_call | solution.py:592
  45.6 3.0 %finish.1 = (f32[4,4,32,32]{3,2,1,0:T(8,128)}, bf16[1024,2,256]{2,1,0:T(2,128)(2,1)}) custom-call(bf16[4,2,16,256]{3,2,1,0:T(8,128)(2,1)} %get-tuple-element.5.fin_hbm, s32[8,128]{1,0:T(8,128)} %get-tuple-element.6.line_hbm, f32[4,32,128]{2,1,0:T(8,128)} %get-tuple-element.7.found_hbm), custom_call_target="tpu_custom_call" | custom-call | tf_op jit(solution)/shard_map/finish/pallas_call | solution.py:668

commit v11 on v9

--- a/solution.py
+++ b/solution.py
@@ -29,10 +29,6 @@
     return jnp.dot(a, b, preferred_element_type=F32)
 
 
-def dot_t(a, b):
-    return lax.dot_general(a, b, (((0,), (0,)), ((), ())), preferred_element_type=F32)
-
-
 def poly_sin_cos(r):
     s = r * r
     sin = r * (1.0 + s * (-1 / 6 + s * (1 / 120 + s * (-1 / 5040 + s * (1 / 362880)))))
@@ -74,7 +70,7 @@
     scores_hbm, rows_hbm, line_hbm,
     scores_ref, line_ref, lines_ref, weights_ref, defocus_ref, sy_ref, sx_ref,
     vbuf, ibuf, split, own, arrived, gather, place_s, place_t,
-    fx, ephase, fy, hs, cx, term, sent, landed, xsend, xrecv, ysend, yrecv, zsend, zrecv,
+    fx, ephase, fy, hs, cx, term, sent, landed, xsend, xsum, xrecv, ysend, yrecv, zsend, zrecv,
     fin, tile_y, zacc, su,
     small_sem, in_sem, out_sem, s_send, s_recv, p_send, p_recv, x_send, x_recv, z_send, z_recv,
     y_send, y_recv, f_send, f_recv,
@@ -202,8 +198,11 @@
     sin_x, cos_x = turns_sin_cos(freq * row_x[0:1])
     sin_y, cos_y = turns_sin_cos(freq * row_y[0:1])
     wide_lane = iota((KS, 128), 1)
-    ephase[0:KS] = jnp.where(wide_lane < NT, cos_y, -sin_y)[:, : 2 * NT].astype(BF16)
-    ephase[KS:] = jnp.where(wide_lane < NT, sin_y, cos_y)[:, : 2 * NT].astype(BF16)
+    e_re = jnp.where(wide_lane < NT, cos_y, -sin_y)[:, : 2 * NT].astype(BF16)
+    e_im = jnp.where(wide_lane < NT, sin_y, cos_y)[:, : 2 * NT].astype(BF16)
+    for block in range(2):
+        ephase[block, 0:128] = e_re[block * 128 : block * 128 + 128]
+        ephase[block, 128:] = e_im[block * 128 : block * 128 + 128]
     t_cos = cos_x.T[0:NT]
     t_sin = sin_x.T[0:NT]
     table = jnp.concatenate([t_cos, t_sin], 1)
@@ -237,12 +236,14 @@
     loads[2].wait()
     loads[3].wait()
     for p in range(P_DEV):
+        sin_p = jnp.broadcast_to(sin_col[:, p : p + 1], (KS, 128))
+        cos_p = jnp.broadcast_to(cos_col[:, p : p + 1], (KS, 128))
         for j in range(2):
             at = slice(j * 128, j * 128 + 128)
             split[...] = ibuf.at[j, p].reshape(2 * KS, 128)[...].astype(F32)
             ctf = (
-                sin_col[:, p : p + 1] * u_row[p : p + 1, at]
-                + cos_col[:, p : p + 1] * v_row[p : p + 1, at]
+                sin_p * u_row[p : p + 1, at]
+                + cos_p * v_row[p : p + 1, at]
             )
             cx[p, 0, :, at] = ctf * split[pl.ds(0, KS, stride=2), :]
             cx[p, 1, :, at] = ctf * split[pl.ds(1, KS, stride=2), :]
@@ -250,12 +251,12 @@
     def placed_term(o):
         for block in range(2):
             at = slice(block * 128, block * 128 + 128)
-            low = slice(KS + block * 128, KS + block * 128 + 128)
             t_re = None
             for p in range(P_DEV):
                 table_h = hs[p * ORIENT + o]
-                g_re = dot(ephase[at], table_h)
-                g_im = dot(ephase[low], table_h)
+                g = dot(ephase[block], table_h)
+                g_re = g[0:128]
+                g_im = g[128:]
                 c_re = cx[p, 0, at]
                 c_im = cx[p, 1, at]
                 if t_re is None:
@@ -278,12 +279,19 @@
             device_id_type=MESH,
         )
 
-    def x_copy(j, k):
+    def x_copy(j, step):
+        ahead = 1 + 2 * j
+        back = 3 - 2 * j
+        src, dst, k = (
+            (xsend.at[j, lax.rem(x + 2, 4)], xrecv.at[j, 0], ahead),
+            (xsend.at[j, lax.rem(x + back, 4)], xrecv.at[j, 1], back),
+            (xsum.at[j], xrecv.at[j, 2], ahead),
+        )[step]
         return pltpu.make_async_remote_copy(
-            src_ref=xsend.at[j, lax.rem(x + k, 4)],
-            dst_ref=xrecv.at[j, x],
-            send_sem=x_send.at[j],
-            recv_sem=x_recv.at[j],
+            src_ref=src,
+            dst_ref=dst,
+            send_sem=x_send.at[j, step],
+            recv_sem=x_recv.at[j, step],
             device_id=x_peer(k),
             device_id_type=MESH,
         )
@@ -343,15 +351,20 @@
         both = (mine + landed[j].astype(F32)).astype(BF16)
         xsend[j] = both.reshape(4, 64, 2 * KS)
 
-        def send_x(k, inner):
-            x_copy(j, k).start()
-            return inner
-
-        lax.fori_loop(1, 4, send_x, 0)
-        xrecv[j, x] = xsend[j, x]
+        x_copy(j, 0).start()
+        x_copy(j, 1).start()
         return carry
 
     lax.fori_loop(0, 2, keep, 0)
+
+    def relay(j, carry):
+        x_copy(j, 0).wait_recv()
+        mine = xsend[j, lax.rem(x + 1 + 2 * j, 4)]
+        xsum[j] = (mine.astype(F32) + xrecv[j, 0].astype(F32)).astype(BF16)
+        x_copy(j, 2).start()
+        return carry
+
+    lax.fori_loop(0, 2, relay, 0)
 
     def wait_rows(n, sem):
         part = arrived.at[0, pl.ds(0, n)]
@@ -368,9 +381,10 @@
             device_id_type=MESH,
         )
 
+    at_s = [owner[o : o + 1] * OWNED + ranks[o] for o in range(ORIENT)]
+    at_s = jnp.concatenate(at_s + at_s, 0).astype(F32).T.astype(jnp.int32)
     for o in range(ORIENT):
-        at_s = owner[o : o + 1] * OWNED + ranks[o]
-        place_s[o] = (iota((KS, KS), 0) == at_s).astype(F32).astype(BF16)
+        place_s[o] = (iota((KS, KS), 1) == at_s[:, o : o + 1]).astype(F32).astype(BF16)
     group = wide_lane // NT
     for o in range(ORIENT):
         cos_o = jnp.where(group == o, cos_x, 0.0).astype(BF16)
@@ -388,7 +402,7 @@
     def correlate(parity, first):
         for j in range(2):
             o = 2 * j + parity
-            su[j] = dot_t(place_s[o], arrived[o].reshape(KS, 2 * KS))
+            su[j] = dot(place_s[o], arrived[o].reshape(KS, 2 * KS))
         for block in range(2):
             at = slice(block * 128, block * 128 + 128)
             for p in range(P_DEV):
@@ -420,13 +434,12 @@
     to_partner.start()
 
     def pass_on(j, carry):
-        pltpu.make_async_copy(
-            xrecv.at[j, pl.ds(0, 3)], xrecv.at[j, pl.ds(0, 3)], x_recv.at[j]
-        ).wait()
+        x_copy(j, 1).wait_recv()
+        x_copy(j, 2).wait_recv()
         for part in range(2):
             at = slice(part * KS, part * KS + KS)
-            total = xrecv[j, 0, :, at].astype(F32)
-            for other in range(1, 4):
+            total = xsend[j, x, :, at].astype(F32)
+            for other in range(1, 3):
                 total += xrecv[j, other, :, at].astype(F32)
             tile_y[:, part * 8 : part * 8 + 8] = total.reshape(YS, 8, KS)
         ysend[j] = tile_y[...].astype(BF16)
@@ -509,9 +522,8 @@
     for j in range(2):
         pair_copy(j).wait_send()
     for j in range(2):
-        pltpu.make_async_copy(
-            xrecv.at[j, pl.ds(0, 3)], xrecv.at[j, pl.ds(0, 3)], x_send.at[j]
-        ).wait()
+        for step in range(3):
+            x_copy(j, step).wait_send()
     for j in range(2):
         pltpu.make_async_copy(
             yrecv.at[j, pl.ds(0, YS - 1)], yrecv.at[j, pl.ds(0, YS - 1)], y_send.at[j]
@@ -599,7 +611,7 @@
             pltpu.VMEM((ORIENT, KS, KS), BF16),
             pltpu.VMEM((ORIENT, KS, KS), BF16),
             pltpu.VMEM((2, 4 * KS, 256), BF16),
-            pltpu.VMEM((2 * KS, 2 * NT), BF16),
+            pltpu.VMEM((2, KS, 2 * NT), BF16),
             pltpu.VMEM((2 * NT, 2 * KS), BF16),
             pltpu.VMEM((P_DEV * ORIENT, 2 * NT, KS), BF16),
             pltpu.VMEM((P_DEV, 2, KS, KS), F32),
@@ -607,7 +619,8 @@
             pltpu.VMEM((2, KS, 2 * KS), BF16),
             pltpu.VMEM((2, KS, 2 * KS), BF16),
             pltpu.VMEM((2, 4, 64, 2 * KS), BF16),
-            pltpu.VMEM((2, 4, 64, 2 * KS), BF16),
+            pltpu.VMEM((2, 64, 2 * KS), BF16),
+            pltpu.VMEM((2, 3, 64, 2 * KS), BF16),
             pltpu.VMEM((2, YS, 16, KS), BF16),
             pltpu.VMEM((2, YS, 16, KS), BF16),
             pltpu.VMEM((2, 16, KS), BF16),
@@ -623,8 +636,8 @@
             dma((5,)),
             dma((2,)),
             dma((2,)),
-            dma((2,)),
-            dma((2,)),
+            dma((2, 3)),
+            dma((2, 3)),
             dma((2,)),
             dma((2,)),
             dma((2,)),

time: 46.3 us -> 46.8 us (1.011)
  Pallas kernels: 45.5 us -> 46 us
    pallas_call x1, Pallas kernels: 42.4 us -> 43 us  [body(): pl.pallas_call(kernel, out_shape=(jax.ShapeDtypeStruct((P_DEV, NT, ORIENT...]
where the time goes in v11:
time: 46.8 us; the launch traced here: 46.6 us
  Pallas kernels  46 us (98%)
  between operations  0.64 us (1%)
    pallas_call x1, Pallas kernels, body(): pl.pallas_call(kernel, out_shape=(jax.ShapeDtypeStruct((P_DEV, NT, ORIENT...  43 us
    pallas_call x1, Pallas kernels, body(): pl.pallas_call(finish, out_shape=(jax.ShapeDtypeStruct((P_DEV, ORIENT, NT...  3.05 us

profile of v11, /device:TPU:1, one launch (start us, length us, event | category | flops | bytes accessed | tf_op | source)
XLA Modules:
  0.0 46.6 jit_solution(1455560007028156245)
XLA Ops:
  0.6 43.0 %cryo.1 = (f32[4,32,128]{2,1,0:T(8,128)}, bf16[4,2,16,256]{3,2,1,0:T(8,128)(2,1)}, s32[8,128]{1,0:T(8,128)}) custom-call(s32[4,256]{1,0:T(4,128)} %lines_hbm.1, f32[512,32]{1,0:T(8,128)} %bitcast.1, f32[4]{0:T(128)} %defocus_hbm.1, s32[32]{0:T(128)} %sy_hbm.1, s32[32]{0:T(128)} %sx_hbm.1, bf16[1024,2,256]{2,1,0:T(2,128)(2,1)} %volume_hbm.1, ...), custom_call_target="tpu_custom_call" | custom-call | tf_op jit(solution)/shard_map/cryo/pallas_call | solution.py:588
  43.6 3.0 %finish.1 = (f32[4,4,32,32]{3,2,1,0:T(8,128)}, bf16[1024,2,256]{2,1,0:T(2,128)(2,1)}) custom-call(bf16[4,2,16,256]{3,2,1,0:T(8,128)(2,1)} %get-tuple-element.5.fin_hbm, s32[8,128]{1,0:T(8,128)} %get-tuple-element.6.line_hbm, f32[4,32,128]{2,1,0:T(8,128)} %get-tuple-element.7.found_hbm), custom_call_target="tpu_custom_call" | custom-call | tf_op jit(solution)/shard_map/finish/pallas_call | solution.py:661

commit v12 on v9

--- a/solution.py
+++ b/solution.py
@@ -29,10 +29,6 @@
     return jnp.dot(a, b, preferred_element_type=F32)
 
 
-def dot_t(a, b):
-    return lax.dot_general(a, b, (((0,), (0,)), ((), ())), preferred_element_type=F32)
-
-
 def poly_sin_cos(r):
     s = r * r
     sin = r * (1.0 + s * (-1 / 6 + s * (1 / 120 + s * (-1 / 5040 + s * (1 / 362880)))))
@@ -75,7 +71,7 @@
     scores_ref, line_ref, lines_ref, weights_ref, defocus_ref, sy_ref, sx_ref,
     vbuf, ibuf, split, own, arrived, gather, place_s, place_t,
     fx, ephase, fy, hs, cx, term, sent, landed, xsend, xrecv, ysend, yrecv, zsend, zrecv,
-    fin, tile_y, zacc, su,
+    fin, tile_y, zacc, su, cq, q,
     small_sem, in_sem, out_sem, s_send, s_recv, p_send, p_recv, x_send, x_recv, z_send, z_recv,
     y_send, y_recv, f_send, f_recv,
 ):
@@ -202,8 +198,11 @@
     sin_x, cos_x = turns_sin_cos(freq * row_x[0:1])
     sin_y, cos_y = turns_sin_cos(freq * row_y[0:1])
     wide_lane = iota((KS, 128), 1)
-    ephase[0:KS] = jnp.where(wide_lane < NT, cos_y, -sin_y)[:, : 2 * NT].astype(BF16)
-    ephase[KS:] = jnp.where(wide_lane < NT, sin_y, cos_y)[:, : 2 * NT].astype(BF16)
+    e_re = jnp.where(wide_lane < NT, cos_y, -sin_y)[:, : 2 * NT].astype(BF16)
+    e_im = jnp.where(wide_lane < NT, sin_y, cos_y)[:, : 2 * NT].astype(BF16)
+    for block in range(2):
+        ephase[block, 0:128] = e_re[block * 128 : block * 128 + 128]
+        ephase[block, 128:] = e_im[block * 128 : block * 128 + 128]
     t_cos = cos_x.T[0:NT]
     t_sin = sin_x.T[0:NT]
     table = jnp.concatenate([t_cos, t_sin], 1)
@@ -237,25 +236,29 @@
     loads[2].wait()
     loads[3].wait()
     for p in range(P_DEV):
+        sin_p = jnp.broadcast_to(sin_col[:, p : p + 1], (KS, 128))
+        cos_p = jnp.broadcast_to(cos_col[:, p : p + 1], (KS, 128))
         for j in range(2):
             at = slice(j * 128, j * 128 + 128)
             split[...] = ibuf.at[j, p].reshape(2 * KS, 128)[...].astype(F32)
             ctf = (
-                sin_col[:, p : p + 1] * u_row[p : p + 1, at]
-                + cos_col[:, p : p + 1] * v_row[p : p + 1, at]
+                sin_p * u_row[p : p + 1, at]
+                + cos_p * v_row[p : p + 1, at]
             )
-            cx[p, 0, :, at] = ctf * split[pl.ds(0, KS, stride=2), :]
-            cx[p, 1, :, at] = ctf * split[pl.ds(1, KS, stride=2), :]
+            for part in range(2):
+                product = ctf * split[pl.ds(part, KS, stride=2), :]
+                cx[p, part, :, at] = product
+                cq[p, part, :, at] = product.astype(BF16)
 
     def placed_term(o):
         for block in range(2):
             at = slice(block * 128, block * 128 + 128)
-            low = slice(KS + block * 128, KS + block * 128 + 128)
             t_re = None
             for p in range(P_DEV):
                 table_h = hs[p * ORIENT + o]
-                g_re = dot(ephase[at], table_h)
-                g_im = dot(ephase[low], table_h)
+                g = dot(ephase[block], table_h)
+                g_re = g[0:128]
+                g_im = g[128:]
                 c_re = cx[p, 0, at]
                 c_im = cx[p, 1, at]
                 if t_re is None:
@@ -368,9 +371,10 @@
             device_id_type=MESH,
         )
 
+    at_s = [owner[o : o + 1] * OWNED + ranks[o] for o in range(ORIENT)]
+    at_s = jnp.concatenate(at_s + at_s, 0).astype(F32).T.astype(jnp.int32)
     for o in range(ORIENT):
-        at_s = owner[o : o + 1] * OWNED + ranks[o]
-        place_s[o] = (iota((KS, KS), 0) == at_s).astype(F32).astype(BF16)
+        place_s[o] = (iota((KS, KS), 1) == at_s[:, o : o + 1]).astype(F32).astype(BF16)
     group = wide_lane // NT
     for o in range(ORIENT):
         cos_o = jnp.where(group == o, cos_x, 0.0).astype(BF16)
@@ -388,23 +392,22 @@
     def correlate(parity, first):
         for j in range(2):
             o = 2 * j + parity
-            su[j] = dot_t(place_s[o], arrived[o].reshape(KS, 2 * KS))
-        for block in range(2):
-            at = slice(block * 128, block * 128 + 128)
-            for p in range(P_DEV):
-                c_re = cx[p, 0, at]
-                c_im = cx[p, 1, at]
-                q = []
+            su[j] = dot(place_s[o], arrived[o].reshape(KS, 2 * KS)).astype(BF16)
+        for p in range(P_DEV):
+            for block in range(2):
+                at = slice(block * 128, block * 128 + 128)
+                c_re = cq[p, 0, at]
+                c_im = cq[p, 1, at]
                 for j in range(2):
                     s_re = su[j, at, 0:KS]
                     s_im = su[j, at, KS:]
-                    q.append((s_re * c_re + s_im * c_im).astype(BF16))
-                    q.append((s_re * c_im - s_im * c_re).astype(BF16))
-                part = dot(jnp.concatenate(q, 1), fx[parity])
-                if first:
-                    zacc[p, at] = part
-                else:
-                    zacc[p, at] += part
+                    q[p, at, 2 * j * KS : (2 * j + 1) * KS] = s_re * c_re + s_im * c_im
+                    q[p, at, (2 * j + 1) * KS : (2 * j + 2) * KS] = s_re * c_im - s_im * c_re
+            part = dot(q[p], fx[parity])
+            if first:
+                zacc[p] = part
+            else:
+                zacc[p] += part
 
     line_row = jnp.concatenate([2 * own_line, 2 * own_line + 1], 0).astype(F32)
     line_row = jnp.broadcast_to(line_row, (128, 128)).T[0:8].astype(jnp.int32)
@@ -599,7 +602,7 @@
             pltpu.VMEM((ORIENT, KS, KS), BF16),
             pltpu.VMEM((ORIENT, KS, KS), BF16),
             pltpu.VMEM((2, 4 * KS, 256), BF16),
-            pltpu.VMEM((2 * KS, 2 * NT), BF16),
+            pltpu.VMEM((2, KS, 2 * NT), BF16),
             pltpu.VMEM((2 * NT, 2 * KS), BF16),
             pltpu.VMEM((P_DEV * ORIENT, 2 * NT, KS), BF16),
             pltpu.VMEM((P_DEV, 2, KS, KS), F32),
@@ -615,7 +618,9 @@
             pltpu.VMEM((4, 2, 16, KS), BF16),
             pltpu.VMEM((YS, 16, KS), F32),
             pltpu.VMEM((P_DEV, KS, 256), F32),
-            pltpu.VMEM((2, KS, 2 * KS), F32),
+            pltpu.VMEM((2, KS, 2 * KS), BF16),
+            pltpu.VMEM((P_DEV, 2, KS, KS), BF16),
+            pltpu.VMEM((P_DEV, KS, 4 * KS), BF16),
             dma((5,)),
             dma((4,)),
             dma((3,)),

time: 46.3 us -> 46.6 us (level)
  no operation moved by 1% of the time
where the time goes in v12:
time: 46.6 us; the launch traced here: 46.5 us
  Pallas kernels  45.8 us (98%)
  between operations  0.64 us (1%)
    pallas_call x1, Pallas kernels, body(): pl.pallas_call(kernel, out_shape=(jax.ShapeDtypeStruct((P_DEV, NT, ORIENT...  42.8 us
    pallas_call x1, Pallas kernels, body(): pl.pallas_call(finish, out_shape=(jax.ShapeDtypeStruct((P_DEV, ORIENT, NT...  3.05 us

profile of v12, /device:TPU:1, one launch (start us, length us, event | category | flops | bytes accessed | tf_op | source)
XLA Modules:
  0.0 46.5 jit_solution(2708095981383289438)
XLA Ops:
  0.6 42.8 %cryo.1 = (f32[4,32,128]{2,1,0:T(8,128)}, bf16[4,2,16,256]{3,2,1,0:T(8,128)(2,1)}, s32[8,128]{1,0:T(8,128)}) custom-call(s32[4,256]{1,0:T(4,128)} %lines_hbm.1, f32[512,32]{1,0:T(8,128)} %bitcast.1, f32[4]{0:T(128)} %defocus_hbm.1, s32[32]{0:T(128)} %sy_hbm.1, s32[32]{0:T(128)} %sx_hbm.1, bf16[1024,2,256]{2,1,0:T(2,128)(2,1)} %volume_hbm.1, ...), custom_call_target="tpu_custom_call" | custom-call | tf_op jit(solution)/shard_map/cryo/pallas_call | solution.py:579
  43.4 3.0 %finish.1 = (f32[4,4,32,32]{3,2,1,0:T(8,128)}, bf16[1024,2,256]{2,1,0:T(2,128)(2,1)}) custom-call(bf16[4,2,16,256]{3,2,1,0:T(8,128)(2,1)} %get-tuple-element.5.fin_hbm, s32[8,128]{1,0:T(8,128)} %get-tuple-element.6.line_hbm, f32[4,32,128]{2,1,0:T(8,128)} %get-tuple-element.7.found_hbm), custom_call_target="tpu_custom_call" | custom-call | tf_op jit(solution)/shard_map/finish/pallas_call | solution.py:653

commit v13 on v12

--- a/solution.py
+++ b/solution.py
@@ -109,7 +109,7 @@
         loads.append(
             pltpu.make_async_copy(images_hbm.at[:, :, :, cols], ibuf.at[j], in_sem.at[2 + j])
         )
-    for load in loads:
+    for load in loads[2:] + loads[:2]:
         load.start()
 
     barrier = pltpu.get_barrier_semaphore()
@@ -171,21 +171,6 @@
             jnp.sum(jnp.where(mine, local[o : o + 1], 0.0), axis=1, keepdims=True)
         )
     own_line = jnp.concatenate(own_line, 0).astype(jnp.int32)
-    o_own = 2 * c + z % 2
-    first_line = own_line[0:OWNED]
-    for o in range(1, ORIENT):
-        first_line = jnp.where(o_own == o, own_line[o * OWNED : (o + 1) * OWNED], first_line)
-    column = iota((OWNED, 2 * LINES), 1)
-    gather[0:OWNED] = (column == 2 * first_line).astype(F32).astype(BF16)
-    gather[OWNED:] = (column == 2 * first_line + 1).astype(F32).astype(BF16)
-
-    for j in range(2):
-        loads[j].wait()
-        picked = dot(gather[...], vbuf.at[j].reshape(2 * LINES, 128)[...]).astype(BF16)
-        for part in range(2):
-            at = slice(part * KS + j * 128, part * KS + j * 128 + 128)
-            own[:, at] = picked[part * OWNED : part * OWNED + OWNED]
-
     small[1].wait()
     small[2].wait()
     lane = iota((8, 128), 1) % NT
@@ -322,6 +307,37 @@
     pair_copy(0).start()
     pair_copy(1).start()
 
+    def keep(j, carry):
+        mine = placed_term(2 * c + j)
+        pair_copy(j).wait_recv()
+        both = (mine + landed[j].astype(F32)).astype(BF16)
+        xsend[j] = both.reshape(4, 64, 2 * KS)
+
+        def send_x(k, inner):
+            x_copy(j, k).start()
+            return inner
+
+        lax.fori_loop(1, 4, send_x, 0)
+        xrecv[j, x] = xsend[j, x]
+        return carry
+
+    lax.fori_loop(0, 2, keep, 0)
+
+    o_own = 2 * c + z % 2
+    first_line = own_line[0:OWNED]
+    for o in range(1, ORIENT):
+        first_line = jnp.where(o_own == o, own_line[o * OWNED : (o + 1) * OWNED], first_line)
+    column = iota((OWNED, 2 * LINES), 1)
+    gather[0:OWNED] = (column == 2 * first_line).astype(F32).astype(BF16)
+    gather[OWNED:] = (column == 2 * first_line + 1).astype(F32).astype(BF16)
+
+    for j in range(2):
+        loads[j].wait()
+        picked = dot(gather[...], vbuf.at[j].reshape(2 * LINES, 128)[...]).astype(BF16)
+        for part in range(2):
+            at = slice(part * KS + j * 128, part * KS + j * 128 + 128)
+            own[:, at] = picked[part * OWNED : part * OWNED + OWNED]
+
     def slab_copy(k):
         return pltpu.make_async_remote_copy(
             src_ref=own,
@@ -338,23 +354,6 @@
 
     lax.fori_loop(1, SLABS, send_slab, 0)
     arrived[o_own, slab] = own[...]
-
-
-    def keep(j, carry):
-        mine = placed_term(2 * c + j)
-        pair_copy(j).wait_recv()
-        both = (mine + landed[j].astype(F32)).astype(BF16)
-        xsend[j] = both.reshape(4, 64, 2 * KS)
-
-        def send_x(k, inner):
-            x_copy(j, k).start()
-            return inner
-
-        lax.fori_loop(1, 4, send_x, 0)
-        xrecv[j, x] = xsend[j, x]
-        return carry
-
-    lax.fori_loop(0, 2, keep, 0)
 
     def wait_rows(n, sem):
         part = arrived.at[0, pl.ds(0, n)]

time: 46.6 us -> 47.8 us (1.026); the launches traced: 46.5 us -> 47.2 us
  Pallas kernels: 45.8 us -> 46.5 us
    pallas_call x1, Pallas kernels: 42.8 us -> 43.5 us  [body(): pl.pallas_call(kernel, out_shape=(jax.ShapeDtypeStruct((P_DEV, NT, ORIENT...]
where the time goes in v13:
time: 47.8 us; the launch traced here: 47.2 us
  Pallas kernels  46.5 us (97%)
  between operations  0.64 us (1%)
    pallas_call x1, Pallas kernels, body(): pl.pallas_call(kernel, out_shape=(jax.ShapeDtypeStruct((P_DEV, NT, ORIENT...  43.5 us
    pallas_call x1, Pallas kernels, body(): pl.pallas_call(finish, out_shape=(jax.ShapeDtypeStruct((P_DEV, ORIENT, NT...  3.05 us

profile of v13, /device:TPU:1, one launch (start us, length us, event | category | flops | bytes accessed | tf_op | source)
XLA Modules:
  0.0 47.2 jit_solution(10225923686515859743)
XLA Ops:
  0.6 43.5 %cryo.1 = (f32[4,32,128]{2,1,0:T(8,128)}, bf16[4,2,16,256]{3,2,1,0:T(8,128)(2,1)}, s32[8,128]{1,0:T(8,128)}) custom-call(s32[4,256]{1,0:T(4,128)} %lines_hbm.1, f32[512,32]{1,0:T(8,128)} %bitcast.1, f32[4]{0:T(128)} %defocus_hbm.1, s32[32]{0:T(128)} %sy_hbm.1, s32[32]{0:T(128)} %sx_hbm.1, bf16[1024,2,256]{2,1,0:T(2,128)(2,1)} %volume_hbm.1, ...), custom_call_target="tpu_custom_call" | custom-call | tf_op jit(solution)/shard_map/cryo/pallas_call | solution.py:578
  44.1 3.0 %finish.1 = (f32[4,4,32,32]{3,2,1,0:T(8,128)}, bf16[1024,2,256]{2,1,0:T(2,128)(2,1)}) custom-call(bf16[4,2,16,256]{3,2,1,0:T(8,128)(2,1)} %get-tuple-element.5.fin_hbm, s32[8,128]{1,0:T(8,128)} %get-tuple-element.6.line_hbm, f32[4,32,128]{2,1,0:T(8,128)} %get-tuple-element.7.found_hbm), custom_call_target="tpu_custom_call" | custom-call | tf_op jit(solution)/shard_map/finish/pallas_call | solution.py:652
